TPU v7x, 256 devices: a whole 4x4x8 slice. The times are simulated.
256 devices in a mesh: chan: 4 (over z_lo), seq: 64 (over x, y, z_hi, core).
Axes of the slice: x: 4, y: 4, z: 8 (z_hi: 2, z_lo: 4; z = z_hi * 4 + z_lo), core: 2. Of those that a mesh axis runs over, the one named last changes fastest.
Arguments:
- ids: int32 [16384], P('seq'), may hold values from 0 to 511
- embed_proj: bfloat16 [512, 3, 4096], P(None, None, 'chan'), may hold values from -6 to 6
- short_filter: float32 [7, 3, 4096], P(None, None, 'chan'), may hold values from -2 to 2
- mr_filter: bfloat16 [256, 128], replicated, may hold values from -0.5 to 0.5
- li_proj: bfloat16 [4096, 3, 4096], P('seq', None, 'chan'), may hold values from -0.09375 to 0.09375
- residue: float32 [256, 16], replicated, may hold values from -1.5 to 1.5
- rate: float32 [256, 16], replicated, may hold values from 0.5 to 512
- out_proj: bfloat16 [4096, 512], P('chan'), may hold values from -0.09375 to 0.09375
Outputs:
- logits: bfloat16 [16384, 512], P('seq', 'chan')
All inputs are finite; a program needn't handle non-finite values.
Results may differ from a plain program's by a relative error of at most 0.015.
Values may be sent and summed in bfloat16 or wider, within the bound.
No kernel may reach another device: no remote copies, remote signals or barrier semaphores. Data moves between devices by JAX's collectives and lax.ppermute only.
A program may use at most 192 MiB of HBM per device.

v0:
```python
import functools

import jax
import jax.numpy as jnp
from jax import lax
from jax.experimental import pallas as pl
from jax.experimental.pallas import tpu as pltpu
from jax.sharding import Mesh
from jax.sharding import PartitionSpec as P

F32 = jnp.float32
BF16 = jnp.bfloat16
GSIZE = 16
NX, NY, NH, NC, NL = 4, 4, 2, 2, 4
NZ = NH * NL
SEQ = ("x", "y", "run", "core")
HALO = 144
HIGHEST = lax.Precision.HIGHEST


def seq_of(x, y, h, c):
    return ((x * NY + y) * NH + h) * NC + c


COORDS = [
    (x, y, h, c) for x in range(NX) for y in range(NY) for h in range(NH) for c in range(NC)
]


def seq_pairs(move):
    return [(seq_of(*a), seq_of(*move(*a))) for a in COORDS]


def from_x(v, j):
    return lax.ppermute(v, SEQ, seq_pairs(lambda x, y, h, c: ((x - j) % NX, y, h, c)))


def from_y(v, j):
    return lax.ppermute(v, SEQ, seq_pairs(lambda x, y, h, c: (x, (y - j) % NY, h, c)))


def from_run(v):
    return lax.ppermute(v, SEQ, seq_pairs(lambda x, y, h, c: (x, y, 1 - h, c)))


def from_core(v):
    return lax.ppermute(v, SEQ, seq_pairs(lambda x, y, h, c: (x, y, h, 1 - c)))


def from_x_before(v, j):
    pairs = [(seq_of(x, y, h, c), seq_of(x + j, y, h, c)) for x, y, h, c in COORDS if x + j < NX]
    return lax.ppermute(v, SEQ, pairs)


def to_z(v, d):
    pairs = []
    for z in range(NZ):
        for x in range(NX):
            for y in range(NY):
                for c in range(NC):
                    t = (z + d) % NZ
                    pairs.append(
                        (
                            (z % NL) * len(COORDS) + seq_of(x, y, z // NL, c),
                            (t % NL) * len(COORDS) + seq_of(x, y, t // NL, c),
                        )
                    )
    return lax.ppermute(v, ("chan",) + SEQ, pairs)


def act_kernel(
    where, ids_ref, emb_ref, sf_ref, mr_ref, keep_ref, send_ref, hot, feats, bands, held
):
    rows = keep_ref.shape[0]
    ext = hot.shape[0]
    step = pl.program_id(0)
    core = where[3]
    yy = lax.rem(where[1] + step, NY)
    wide = pl.ds(pl.multiple_of(yy * 256, 256), 256)

    @pl.when(step == 0)
    def _():
        col = lax.broadcasted_iota(jnp.int32, hot.shape, 1)
        hot[...] = jnp.where(ids_ref[...] == col, 1.0, 0.0).astype(BF16)

    for j in range(3):
        feats[j] = jnp.dot(hot[...], emb_ref[j, :, wide], preferred_element_type=F32)

    reach = 128
    group = (lax.broadcasted_iota(jnp.int32, (128, 256), 1) // GSIZE) % 8
    for b in range(2):
        cols = slice(b * 128, (b + 1) * 128)
        lanes = pl.ds(pl.multiple_of(yy * 256 + b * 128, 128), 128)

        def short(j, start, n, cols=cols, lanes=lanes):
            total = sf_ref[j, 0:1, lanes] * feats[j, start : start + n, cols]
            for k in range(1, 7):
                tap = sf_ref[j, k : k + 1, lanes]
                total = total + tap * feats[j, start - k : start - k + n, cols]
            return total

        first = ext - rows - reach
        gated = (short(0, first, rows + reach) * short(1, first, rows + reach)).astype(BF16)
        window = jnp.concatenate([gated[:256], gated[128:384]], axis=1)
        filt = mr_ref[pl.ds(pl.multiple_of(yy * 16 + b * 8, 8), 8), :]
        for g in range(8):
            base = jnp.broadcast_to(filt[g : g + 1, :], (128, 256))
            bands[g * 128 : (g + 1) * 128, :] = pltpu.roll(
                base, 0, 1, stride=1, stride_axis=0
            ).astype(BF16)
        both = jnp.dot(bands[...], window, preferred_element_type=F32)
        medium = both[:128]
        for g in range(1, 8):
            medium = jnp.where(group == g, both[g * 128 : (g + 1) * 128], medium)
        v1 = short(2, ext - rows, rows)
        out = jnp.concatenate([v1[:128] * medium[:, :128], v1[128:] * medium[:, 128:]], axis=0)

        @pl.when(lax.rem(step, 2) == 0)
        def _(out=out, b=b):
            held[b] = out

        @pl.when(lax.rem(step, 2) == 1)
        def _(out=out, b=b):
            even = jnp.concatenate([held[b, :, :64], out[:, :64]], axis=1)
            odd = jnp.concatenate([held[b, :, 64:], out[:, 64:]], axis=1)
            to = pl.ds(pl.multiple_of(b * 256 + (step // 2) * 128, 128), 128)
            keep_ref[:, to] = jnp.where(core == 0, even, odd).astype(BF16)
            send_ref[:, to] = jnp.where(core == 0, odd, even).astype(BF16)


def activations(where, ids, emb, sf, mr_rows):
    ext = ids.shape[0]
    return pl.pallas_call(
        act_kernel,
        grid=(4,),
        out_shape=(jax.ShapeDtypeStruct((256, 512), BF16),) * 2,
        in_specs=[
            pl.BlockSpec(memory_space=pltpu.SMEM),
            pl.BlockSpec(memory_space=pltpu.VMEM),
            pl.BlockSpec(memory_space=pltpu.VMEM),
            pl.BlockSpec(memory_space=pltpu.VMEM),
            pl.BlockSpec(memory_space=pltpu.VMEM),
        ],
        out_specs=(pl.BlockSpec(memory_space=pltpu.VMEM),) * 2,
        scratch_shapes=[
            pltpu.VMEM((ext, 512), BF16),
            pltpu.VMEM((3, ext, 256), F32),
            pltpu.VMEM((1024, 256), BF16),
            pltpu.VMEM((2, 256, 128), F32),
        ],
        compiler_params=pltpu.CompilerParams(vmem_limit_bytes=12 * 2**20),
        cost_estimate=pl.CostEstimate(flops=4 * 10**9, bytes_accessed=8 * 10**6, transcendentals=0),
    )(where, ids, emb, sf, mr_rows)


def toeplitz_kernel(h_ref, out_ref):
    for g in range(8):
        base = jnp.broadcast_to(h_ref[g : g + 1, :], (256, 512))
        out_ref[g] = pltpu.roll(base, 0, 1, stride=1, stride_axis=0)[:, :256].astype(BF16)


def toeplitz(base_rows):
    groups = base_rows.shape[0]
    return pl.pallas_call(
        toeplitz_kernel,
        grid=(groups // 8,),
        out_shape=jax.ShapeDtypeStruct((groups, 256, 256), BF16),
        in_specs=[pl.BlockSpec((8, 512), lambda i: (i, 0))],
        out_specs=pl.BlockSpec((8, 256, 256), lambda i: (i, 0, 0)),
        compiler_params=pltpu.CompilerParams(vmem_limit_bytes=12 * 2**20),
        cost_estimate=pl.CostEstimate(flops=10**7, bytes_accessed=4 * 10**6, transcendentals=0),
    )(base_rows)


def block_place(where, d):
    zz = lax.rem(where[4] + d + NZ, NZ)
    rows = pl.multiple_of((zz // NL) * 256, 256)
    lanes = pl.multiple_of(lax.rem(zz, NL) * 512, 512)
    return pl.ds(rows, 256), pl.ds(lanes, 512)


def gather_kernel(steps, plan, halves, where, *refs):
    n_in = len(steps) + len(plan)
    sources = refs[:n_in]
    outs = 4 if halves else 2
    a_ref, w_ref = refs[-1 - outs], refs[-outs]
    sem = refs[-1]
    x, h = where[0], where[2]
    copies = []
    for src, (d, first, count) in zip(sources, steps):
        rows, lanes = block_place(where, d)
        for p in range(count):
            copies.append((src.at[pl.ds(p * 256, 256), :], a_ref.at[first + p, rows, lanes]))
    for src, (own_run, at) in zip(sources[len(steps) :], plan):
        run = h if own_run else 1 - h
        for other in range(4):
            j, k = (other, at) if own_run else (at, other)
            row = lax.rem(x + j, NX) * 512 + run * 256 + k * 64
            rows = pl.ds(pl.multiple_of(row, 64), 64)
            copies.append((src.at[other], w_ref.at[:, rows, :]))
    if halves:
        copies.append((sources[0].at[pl.ds(0, 256), :], refs[-3]))
        copies.append((sources[1].at[pl.ds(256, 256), :], refs[-2]))
    copies = [pltpu.make_async_copy(a, b, sem.at[n]) for n, (a, b) in enumerate(copies)]
    for copy in copies:
        copy.start()
    for copy in copies:
        copy.wait()


def gather(where, full, blocks, pieces, halves=False):
    steps = [b[:3] for b in blocks]
    plan = [(own_run, at) for own_run, at, _ in pieces]
    operands = [b[3] for b in blocks] + [v for _, _, v in pieces]
    vmem = pl.BlockSpec(memory_space=pltpu.VMEM)
    alias = {}
    if full is not None:
        alias = {1 + len(operands): 0, 2 + len(operands): 1}
        operands += list(full)
    n_copies = sum(c for _, _, c in steps) + 4 * len(plan) + 2 * halves
    shapes = (
        jax.ShapeDtypeStruct((2, 512, 2048), BF16),
        jax.ShapeDtypeStruct((3, 2048, 512), BF16),
    )
    shapes += (jax.ShapeDtypeStruct((256, 512), BF16),) * (2 * halves)
    return pl.pallas_call(
        functools.partial(gather_kernel, steps, plan, halves),
        out_shape=shapes,
        in_specs=[pl.BlockSpec(memory_space=pltpu.SMEM)] + [vmem] * len(operands),
        out_specs=(vmem,) * len(shapes),
        scratch_shapes=[pltpu.SemaphoreType.DMA((n_copies,))],
        input_output_aliases=alias,
        compiler_params=pltpu.CompilerParams(vmem_limit_bytes=4 * 2**20),
        cost_estimate=pl.CostEstimate(flops=10**6, bytes_accessed=6 * 10**6, transcendentals=0),
    )(where, *operands)


def li_kernel(which, a_ref, w_ref, out_ref):
    for t in range(3):

        def step(m, _, t=t):
            rows = pl.ds(pl.multiple_of(m * 256, 256), 256)
            out_ref[t, rows, :] = jnp.dot(
                a_ref[which, rows, :], w_ref[t], preferred_element_type=F32
            ).astype(out_ref.dtype)
            return 0

        lax.fori_loop(0, 2, step, 0)


def li_terms(which, a_full, w_full):
    vmem = pl.BlockSpec(memory_space=pltpu.VMEM)
    return pl.pallas_call(
        functools.partial(li_kernel, which),
        out_shape=jax.ShapeDtypeStruct((3, 512, 512), BF16 if which else F32),
        in_specs=[vmem] * 2,
        out_specs=vmem,
        compiler_params=pltpu.CompilerParams(vmem_limit_bytes=8 * 2**20),
        cost_estimate=pl.CostEstimate(
            flops=33 * 10**8, bytes_accessed=10 * 10**6, transcendentals=0
        ),
    )(a_full, w_full)


def states_kernel(own_ref, got_ref, fade_ref, q_ref, mixed_ref, state_ref):
    q_ref[...] = own_ref[0] + got_ref[0].astype(F32)
    group = lax.broadcasted_iota(jnp.int32, (16, 128), 1) // GSIZE
    for b in range(4):
        cols = slice(b * 128, (b + 1) * 128)
        fade = fade_ref[cols, :]
        high = fade.astype(BF16)
        low = (fade - high.astype(F32)).astype(BF16)
        for m in range(2):
            rows = slice(m * 256, (m + 1) * 256)
            k2 = own_ref[1, rows, cols] + got_ref[1, rows, cols].astype(F32)
            v2 = own_ref[2, rows, cols] + got_ref[2, rows, cols].astype(F32)
            block = (k2 * v2).astype(BF16)
            mixed_ref[rows, cols] = block
            full = jnp.dot(high, block, preferred_element_type=F32) + jnp.dot(
                low, block, preferred_element_type=F32
            )
            state = full[:16]
            for g in range(1, 8):
                state = jnp.where(group == g, full[g * 16 : (g + 1) * 16], state)
            state_ref[m, :, cols] = state


def block_states(own, got, fade):
    vmem = pl.BlockSpec(memory_space=pltpu.VMEM)
    return pl.pallas_call(
        states_kernel,
        out_shape=(
            jax.ShapeDtypeStruct((512, 512), F32),
            jax.ShapeDtypeStruct((512, 512), BF16),
            jax.ShapeDtypeStruct((2, 16, 512), F32),
        ),
        in_specs=[vmem] * 3,
        out_specs=(vmem,) * 3,
        compiler_params=pltpu.CompilerParams(vmem_limit_bytes=12 * 2**20),
        cost_estimate=pl.CostEstimate(flops=5 * 10**8, bytes_accessed=5 * 10**6, transcendentals=0),
    )(own, got, fade)


def inner_kernel(x_ref, t_ref, out_ref):
    both = jnp.concatenate([x_ref[:256, :], x_ref[256:, :]], axis=1)
    group = (lax.broadcasted_iota(jnp.int32, (256, 256), 1) // GSIZE) % 8
    total = jnp.dot(t_ref[0], both, preferred_element_type=F32)
    for g in range(1, 8):
        total = jnp.where(
            group == g, jnp.dot(t_ref[g], both, preferred_element_type=F32), total
        )
    out_ref[:256, :] = total[:, :128]
    out_ref[256:, :] = total[:, 128:]


def inner(mixed, blocks):
    return pl.pallas_call(
        inner_kernel,
        grid=(4,),
        out_shape=jax.ShapeDtypeStruct((512, 512), F32),
        in_specs=[
            pl.BlockSpec((512, 128), lambda i: (0, i)),
            pl.BlockSpec((8, 256, 256), lambda i: (i, 0, 0)),
        ],
        out_specs=pl.BlockSpec((512, 128), lambda i: (0, i)),
        compiler_params=pltpu.CompilerParams(vmem_limit_bytes=12 * 2**20),
        cost_estimate=pl.CostEstimate(
            flops=43 * 10**8, bytes_accessed=6 * 10**6, transcendentals=0
        ),
    )(mixed, blocks)


def logits_kernel(start_ref, inner_ref, q_ref, log_ref, coef_ref, proj_ref, out_ref, li_out):
    step = (lax.broadcasted_iota(jnp.int32, (256, 128), 0) + 1).astype(F32)
    row_group = lax.broadcasted_iota(jnp.int32, (128, 128), 0) // 16
    col_group = lax.broadcasted_iota(jnp.int32, (128, 128), 1) // GSIZE
    for b in range(4):
        cols = slice(b * 128, (b + 1) * 128)
        lead = coef_ref[:, cols] * jnp.exp(step * log_ref[:, cols])
        for m in range(2):
            tiled = jnp.concatenate([start_ref[m, :, cols]] * 8, axis=0)
            diag = jnp.where(row_group == col_group, tiled, 0.0)
            cross = jnp.dot(lead, diag, precision=HIGHEST, preferred_element_type=F32)
            rows = slice(m * 256, (m + 1) * 256)
            li_out[rows, cols] = (
                q_ref[rows, cols] * (inner_ref[rows, cols] + cross)
            ).astype(BF16)
    for m in range(2):
        part = jnp.dot(
            li_out[m * 256 : (m + 1) * 256, :], proj_ref[...], preferred_element_type=F32
        )
        for v in range(NL):
            out_ref[m * NL + v] = part[:, v * 128 : (v + 1) * 128].astype(BF16)


def logit_terms(start, inside, q2, log_row, coef_row, proj):
    vmem = pl.BlockSpec(memory_space=pltpu.VMEM)
    return pl.pallas_call(
        logits_kernel,
        out_shape=jax.ShapeDtypeStruct((NZ, 256, 128), BF16),
        in_specs=[vmem] * 6,
        out_specs=vmem,
        scratch_shapes=[pltpu.VMEM((512, 512), BF16)],
        compiler_params=pltpu.CompilerParams(vmem_limit_bytes=12 * 2**20),
        cost_estimate=pl.CostEstimate(
            flops=10**9, bytes_accessed=4 * 10**6, transcendentals=10**5
        ),
    )(start, inside, q2, log_row, coef_row, proj)


def shards(ids, embed_proj, short_filter, mr_filter, li_proj, residue, rate, out_proj):
    seq = lax.axis_index(SEQ)
    chan = lax.axis_index("chan")
    x, y, h, c = seq // 16, (seq // 4) % 4, (seq // 2) % 2, seq % 2
    z = h * NL + chan
    where = jnp.stack([x, y, h, c, z]).astype(jnp.int32)
    total_len = ids.shape[0] * lax.axis_size(SEQ)
    tie = lax.optimization_barrier

    halo = lax.ppermute(
        ids[ids.shape[0] - HALO :] + 1, SEQ, [(i, i + 1) for i in range(len(COORDS) - 1)]
    )
    weights = jnp.transpose(li_proj, (1, 0, 2))
    mine = lax.dynamic_slice_in_dim(weights, h * 512, 512, 2)
    theirs = lax.dynamic_slice_in_dim(weights, (1 - h) * 512, 512, 2)
    rows_b = from_run(theirs)
    ext_ids = jnp.concatenate([halo - 1, ids])[:, None]
    emb = jnp.transpose(embed_proj, (1, 0, 2))
    taps = jnp.transpose(short_filter, (1, 0, 2))
    filt = lax.dynamic_slice_in_dim(mr_filter, chan * 64, 64, 0).astype(F32)
    mr_rows = jnp.pad(filt[:, ::-1], ((0, 0), (1, 127)))
    keep, send = activations(where, ext_ids, emb, taps, mr_rows)
    keep, send, mine, rows_b = tie((keep, send, mine, rows_b))
    rate, residue, out_proj, keep = tie((rate, residue, out_proj, keep))
    first = chan * 64 + h * 32
    log_all = -lax.dynamic_slice_in_dim(rate, first, 32, 0) / total_len
    coef = lax.dynamic_slice_in_dim(residue, first, 32, 0) * jnp.sqrt(-jnp.expm1(2.0 * log_all))
    lag = (512 - jnp.arange(512)) % 512
    power = jnp.exp(lag.astype(F32)[None, None, :] * log_all[:, :, None])
    base_rows = jnp.where(lag[None, :] < 256, jnp.sum(coef[:, :, None] * power, axis=1), 0.0)
    blocks = toeplitz(base_rows)
    log_row = log_all.reshape(1, 512)
    coef_row = coef.reshape(1, 512)
    fade = jnp.exp(log_all.reshape(512, 1) * (255 - jnp.arange(256)).astype(F32)[None, :])
    log_ch = tie(jnp.repeat(log_all.T, GSIZE, axis=1))

    def decay(steps, keep=True):
        return jnp.where(keep, jnp.exp(steps * log_ch), 0.0)

    rows_of = 4.0 * ids.shape[0]
    one, row_step = decay(256.0), decay(4096.0)
    to_row = decay(rows_of * y.astype(F32))
    before = [decay(rows_of * (d - 1), d <= y) for d in (1, 2, 3)]
    within = [decay(rows_of * (3 - (y - d) % 4).astype(F32)) for d in range(4)]
    proj = lax.dynamic_slice_in_dim(out_proj, h * 512, 512, 0)
    own = jnp.concatenate([keep, from_core(send)], axis=0)

    a_x = jnp.stack([mine] + [from_x(mine, j) for j in (1, 2, 3)])
    b_y = jnp.stack([rows_b] + [from_y(rows_b, k) for k in (1, 2, 3)])
    up1, down1 = to_z(own, 1), to_z(own, -1)
    params = (fade, one, row_step, to_row, before, within, log_row, coef_row, proj, blocks)
    up1, down1, a_x, b_y, params = tie((up1, down1, a_x, b_y, params))
    fade, one, row_step, to_row, before, within, log_row, coef_row, proj, blocks = params
    full = gather(where, None, [(0, 0, 2, own)], [(True, 0, a_x), (False, 0, b_y)])
    up2, down2 = to_z(up1, 1), to_z(down1, -1)
    x2, y1, y3 = from_x(b_y, 2), from_y(a_x, 1), from_y(a_x, 3)
    full = gather(where, full, [(-1, 0, 2, up1), (1, 0, 2, down1)], [])
    up2, down2, x2, y1, y3, a_x, b_y, full = tie((up2, down2, x2, y1, y3, a_x, b_y, full))
    up3, down3 = to_z(up2, 1), to_z(down2, -1)
    x1, x3, y2 = from_x(b_y, 1), from_x(b_y, 3), from_y(a_x, 2)
    full = gather(
        where, full, [(-2, 0, 2, up2), (2, 0, 2, down2)], [(False, 2, x2), (True, 1, y1), (True, 3, y3)]
    )
    up3, down3, x1, x3, y2, full = tie((up3, down3, x1, x3, y2, full))
    *full, top, bottom = gather(where, full, [(-3, 0, 2, up3), (3, 0, 2, down3)], [], True)
    up4, down4 = to_z(top, 1), to_z(bottom, -1)
    full = gather(where, full, [], [(False, 1, x1), (False, 3, x3), (True, 2, y2)])
    full = gather(where, full, [(-4, 0, 1, up4), (4, 1, 1, down4)], [])

    give = li_terms(1, *full)
    got = from_core(give)
    have = li_terms(0, *full)
    q2, mixed, states = block_states(have, got, fade)
    inside = inner(mixed, blocks)

    other = from_core(states)
    early = jnp.where(c == 0, states, other)
    late = jnp.where(c == 0, other, states)
    s0, s1, s2, s3 = early[0], late[0], early[1], late[1]
    total = s3 + one * (s2 + one * (s1 + one * s0))
    along_y = [total] + [from_y(total, k) for k in (3, 2, 1)]
    row_total = sum(within[d] * along_y[d] for d in range(4))
    before_y = sum(before[d - 1] * along_y[d] for d in (1, 2, 3))
    before_x = from_x_before(row_total, 1) + row_step * (
        from_x_before(row_total, 2) + row_step * from_x_before(row_total, 3)
    )
    at = before_y + to_row * before_x
    at1 = s0 + one * at
    at2 = s1 + one * at1
    at3 = s2 + one * at2
    start = jnp.stack([jnp.where(c == 0, at, at1), jnp.where(c == 0, at2, at3)])

    terms = logit_terms(start, inside, q2, log_row, coef_row, proj)
    terms = lax.all_to_all(terms, ("run", "chan"), 0, 0, tiled=True)
    return jnp.sum(terms.astype(F32), axis=0).astype(BF16)


def solution(mesh):
    chips = Mesh(mesh.devices.reshape(NL, NX, NY, NH, NC), ("chan",) + SEQ)
    in_specs = (
        P(SEQ),
        P(None, None, "chan"),
        P(None, None, "chan"),
        P(),
        P(SEQ, None, "chan"),
        P(),
        P(),
        P("chan", None),
    )
    out_specs = P(SEQ, "chan")
    return jax.shard_map(shards, mesh=chips, in_specs=in_specs, out_specs=out_specs, check_vma=False)
```

profile of v0, /device:TPU:8, one launch (start us, length us, event | category | flops | bytes accessed | tf_op | source)
XLA Modules:
  0.0 162.7 jit_solution(9391727940038348278)
XLA Ops:
  3.9 7.3 %collective-permute-start.1 = (bf16[3,64,512]{2,1,0:T(8,128)(2,1)S(1)}, bf16[3,64,512]{2,1,0:T(8,128)(2,1)S(1)}, u32[]{:S(2)}, u32[]{:S(2)}) collective-permute-start(bf16[3,64,512]{2,1,0:T(8,128)(2,1)S(1)} %get-tuple-element.131), channel_id=1, source_target_pairs={{0,2},{1,3},{2,0},{3,1},{4,6},{5,7},{6,4},{7,5},{8,10},{9,11},{10,... | collective-permute-start | bytes 589832 | tf_op jit(solution)/shard_map/ppermute | solution.py:43
  15.9 8.7 %shard_map.82 = (bf16[256,512]{1,0:T(8,128)(2,1)S(1)}, bf16[256,512]{1,0:T(8,128)(2,1)S(1)}) custom-call(s32[5]{0:T(128)S(1)} %stack.62.where, s32[400,1]{1,0:T(8,128)S(1)} %copy.29.ids_ref, bf16[3,512,1024]{2,1,0:T(8,128)(2,1)S(1)} %bitcast.51, f32[3,7,1024]{2,1,0:T(8,128)S(1)} %bitcast.52, f32[64,256]{1,0:T(8,128)S(1)} %pad.4.mr_ref), custom_call_target="tpu_custom_call" | custom-call | flops 4000000000 | bytes 8000000 | tf_op jit(solution)/shard_map/pallas_call | solution.py:133
  25.2 2.6 %collective-permute-start.9 = (bf16[3,64,512]{2,1,0:T(8,128)(2,1)S(1)}, bf16[3,64,512]{2,1,0:T(8,128)(2,1)S(1)}, u32[]{:S(2)}, u32[]{:S(2)}) collective-permute-start(bf16[3,64,512]{2,1,0:T(8,128)(2,1)S(1)} %collective-permute-done.1), channel_id=1, source_target_pairs={{0,8},{1,9},{2,10},{3,11},{4,12},{5,13},{6,14},{7,15},{8,0},{9,1},... | collective-permute-start | bytes 589832 | tf_op jit(solution)/shard_map/ppermute | solution.py:39
  35.6 2.6 %collective-permute-start.4 = (bf16[512,512]{1,0:T(8,128)(2,1)S(1)}, bf16[512,512]{1,0:T(8,128)(2,1)S(1)}, u32[]{:S(2)}, u32[]{:S(2)}) collective-permute-start(bf16[512,512]{1,0:T(8,128)(2,1)S(1)} %constant_dynamic-update-slice_fusion.refs_0_), channel_id=1, source_target_pairs={{0,194},{1,195},{4,198},{5,199},{8,202},{9,203},{12,206},{13,207},... | collective-permute-start | bytes 1572872 | tf_op jit(solution)/shard_map/ppermute | solution.py:68
  39.0 2.8 %collective-permute-start.5 = (bf16[3,64,512]{2,1,0:T(8,128)(2,1)S(1)}, bf16[3,64,512]{2,1,0:T(8,128)(2,1)S(1)}, u32[]{:S(2)}, u32[]{:S(2)}) collective-permute-start(bf16[3,64,512]{2,1,0:T(8,128)(2,1)S(1)} %get-tuple-element.72), channel_id=1, source_target_pairs={{0,48},{1,49},{2,50},{3,51},{4,52},{5,53},{6,54},{7,55},{8,56},{9,... | collective-permute-start | bytes 589832 | tf_op jit(solution)/shard_map/ppermute | solution.py:35
  43.6 6.6 %collective-permute-done.5 = bf16[3,64,512]{2,1,0:T(8,128)(2,1)S(1)} collective-permute-done((bf16[3,64,512]{2,1,0:T(8,128)(2,1)S(1)}, bf16[3,64,512]{2,1,0:T(8,128)(2,1)S(1)}, u32[]{:S(2)}, u32[]{:S(2)}) %collective-permute-start.5) | collective-permute-done | bytes 196640 | tf_op jit(solution)/shard_map/ppermute | solution.py:35
  51.1 2.7 %collective-permute-done.7 = bf16[3,64,512]{2,1,0:T(8,128)(2,1)S(1)} collective-permute-done((bf16[3,64,512]{2,1,0:T(8,128)(2,1)S(1)}, bf16[3,64,512]{2,1,0:T(8,128)(2,1)S(1)}, u32[]{:S(2)}, u32[]{:S(2)}) %collective-permute-start.7) | collective-permute-done | bytes 196640 | tf_op jit(solution)/shard_map/ppermute | solution.py:35
  56.9 3.2 %collective-permute-start.12 = (bf16[512,512]{1,0:T(8,128)(2,1)S(1)}, bf16[512,512]{1,0:T(8,128)(2,1)S(1)}, u32[]{:S(2)}, u32[]{:S(2)}) collective-permute-start(bf16[512,512]{1,0:T(8,128)(2,1)S(1)} %collective-permute-done.4.refs_1_), channel_id=1, source_target_pairs={{0,194},{1,195},{4,198},{5,199},{8,202},{9,203},{12,206},{13,207},... | collective-permute-start | bytes 1572872 | tf_op jit(solution)/shard_map/ppermute | solution.py:68
  62.3 8.9 %collective-permute-done.11.refs_0_ = bf16[512,512]{1,0:T(8,128)(2,1)S(1)} collective-permute-done((bf16[512,512]{1,0:T(8,128)(2,1)S(1)}, bf16[512,512]{1,0:T(8,128)(2,1)S(1)}, u32[]{:S(2)}, u32[]{:S(2)}) %collective-permute-start.11) | collective-permute-done | bytes 524320 | tf_op jit(solution)/shard_map/ppermute | solution.py:68
  71.2 3.9 %collective-permute-done.13.refs_2_ = bf16[4,3,64,512]{3,2,1,0:T(8,128)(2,1)S(1)} collective-permute-done((bf16[4,3,64,512]{3,2,1,0:T(8,128)(2,1)S(1)}, bf16[4,3,64,512]{3,2,1,0:T(8,128)(2,1)S(1)}, u32[]{:S(2)}, u32[]{:S(2)}) %collective-permute-start.13) | collective-permute-done | bytes 786464 | tf_op jit(solution)/shard_map/ppermute | solution.py:35
  75.1 2.0 %collective-permute-start.19 = (bf16[4,3,64,512]{3,2,1,0:T(8,128)(2,1)S(1)}, bf16[4,3,64,512]{3,2,1,0:T(8,128)(2,1)S(1)}, u32[]{:S(2)}, u32[]{:S(2)}) collective-permute-start(bf16[4,3,64,512]{3,2,1,0:T(8,128)(2,1)S(1)} %pad_maximum_fusion.1.refs_2_), channel_id=1, source_target_pairs={{0,16},{1,17},{2,18},{3,19},{4,20},{5,21},{6,22},{7,23},{8,24},{9,... | collective-permute-start | bytes 2359304 | tf_op jit(solution)/shard_map/ppermute | solution.py:35
  78.6 3.3 %collective-permute-start.17 = (bf16[512,512]{1,0:T(8,128)(2,1)S(1)}, bf16[512,512]{1,0:T(8,128)(2,1)S(1)}, u32[]{:S(2)}, u32[]{:S(2)}) collective-permute-start(bf16[512,512]{1,0:T(8,128)(2,1)S(1)} %collective-permute-done.12.refs_1_), channel_id=1, source_target_pairs={{0,194},{1,195},{4,198},{5,199},{8,202},{9,203},{12,206},{13,207},... | collective-permute-start | bytes 1572872 | tf_op jit(solution)/shard_map/ppermute | solution.py:68
  81.8 2.1 %shard_map.86 = (bf16[2,512,2048]{2,1,0:T(8,128)(2,1)S(1)}, bf16[3,2048,512]{2,1,0:T(8,128)(2,1)S(1)}) custom-call(s32[5]{0:T(128)S(1)} %stack.62.where, bf16[512,512]{1,0:T(8,128)(2,1)S(1)} %collective-permute-done.11.refs_0_, bf16[512,512]{1,0:T(8,128)(2,1)S(1)} %collective-permute-done.12.refs_1_, ...), custom_call_target="tpu_custom_call", output_to_operand_aliasing={{0}: (6, {}), {1}: (7, {})} | custom-call | flops 1000000 | bytes 6000000 | tf_op jit(solution)/shard_map/pallas_call | solution.py:226
  83.9 8.1 %collective-permute-done.16.refs_0_ = bf16[512,512]{1,0:T(8,128)(2,1)S(1)} collective-permute-done((bf16[512,512]{1,0:T(8,128)(2,1)S(1)}, bf16[512,512]{1,0:T(8,128)(2,1)S(1)}, u32[]{:S(2)}, u32[]{:S(2)}) %collective-permute-start.16) | collective-permute-done | bytes 524320 | tf_op jit(solution)/shard_map/ppermute | solution.py:68
  97.5 3.2 %collective-permute-start.22 = (bf16[256,512]{1,0:T(8,128)(2,1)S(1)}, bf16[256,512]{1,0:T(8,128)(2,1)S(1)}, u32[]{:S(2)}, u32[]{:S(2)}) collective-permute-start(bf16[256,512]{1,0:T(8,128)(2,1)S(1)} %get-tuple-element.102), channel_id=1, source_target_pairs={{0,194},{1,195},{4,198},{5,199},{8,202},{9,203},{12,206},{13,207},... | collective-permute-start | bytes 786440 | tf_op jit(solution)/shard_map/ppermute | solution.py:68
  102.4 2.6 %collective-permute-done.21.refs_0_ = bf16[256,512]{1,0:T(8,128)(2,1)S(1)} collective-permute-done((bf16[256,512]{1,0:T(8,128)(2,1)S(1)}, bf16[256,512]{1,0:T(8,128)(2,1)S(1)}, u32[]{:S(2)}, u32[]{:S(2)}) %collective-permute-start.21) | collective-permute-done | bytes 262176 | tf_op jit(solution)/shard_map/ppermute | solution.py:68
  105.7 4.2 %shard_map.91 = bf16[3,512,512]{2,1,0:T(8,128)(2,1)S(1)} custom-call(bf16[2,512,2048]{2,1,0:T(8,128)(2,1)S(1)} %get-tuple-element.110.a_ref, bf16[3,2048,512]{2,1,0:T(8,128)(2,1)S(1)} %get-tuple-element.111.w_ref), custom_call_target="tpu_custom_call" | custom-call | flops 3300000000 | bytes 10000000 | tf_op jit(solution)/shard_map/pallas_call | solution.py:253
  110.1 4.2 %shard_map.90.own_ref = f32[3,512,512]{2,1,0:T(8,128)S(1)} custom-call(bf16[2,512,2048]{2,1,0:T(8,128)(2,1)S(1)} %get-tuple-element.110.a_ref, bf16[3,2048,512]{2,1,0:T(8,128)(2,1)S(1)} %get-tuple-element.111.w_ref), custom_call_target="tpu_custom_call" | custom-call | flops 3300000000 | bytes 10000000 | tf_op jit(solution)/shard_map/pallas_call | solution.py:253
  117.6 3.5 %collective-permute-start.26 = (f32[16,512]{1,0:T(8,128)S(1)}, f32[16,512]{1,0:T(8,128)S(1)}, u32[]{:S(2)}, u32[]{:S(2)}) collective-permute-start(f32[16,512]{1,0:T(8,128)S(1)} %fusion), channel_id=1, source_target_pairs={{0,8},{1,9},{2,10},{3,11},{4,12},{5,13},{6,14},{7,15},{8,0},{9,1},... | collective-permute-start | bytes 98312 | tf_op jit(solution)/shard_map/ppermute | solution.py:39
  121.2 2.2 %collective-permute-done.26 = f32[16,512]{1,0:T(8,128)S(1)} collective-permute-done((f32[16,512]{1,0:T(8,128)S(1)}, f32[16,512]{1,0:T(8,128)S(1)}, u32[]{:S(2)}, u32[]{:S(2)}) %collective-permute-start.26) | collective-permute-done | bytes 32800 | tf_op jit(solution)/shard_map/ppermute | solution.py:39
  125.1 2.8 %collective-permute-start.28 = (f32[16,512]{1,0:T(8,128)S(1)}, f32[16,512]{1,0:T(8,128)S(1)}, u32[]{:S(2)}, u32[]{:S(2)}) collective-permute-start(f32[16,512]{1,0:T(8,128)S(1)} %multiply_add_fusion.2), channel_id=1, source_target_pairs={{0,16},{1,17},{2,18},{3,19},{4,20},{5,21},{6,22},{7,23},{8,24},{9,... | collective-permute-start | bytes 98312 | tf_op jit(solution)/shard_map/ppermute | solution.py:52
  127.9 4.0 %collective-permute-start.29 = (f32[16,512]{1,0:T(8,128)S(1)}, f32[16,512]{1,0:T(8,128)S(1)}, u32[]{:S(2)}, u32[]{:S(2)}) collective-permute-start(f32[16,512]{1,0:T(8,128)S(1)} %multiply_add_fusion.2), channel_id=1, source_target_pairs={{0,32},{1,33},{2,34},{3,35},{4,36},{5,37},{6,38},{7,39},{8,40},{9,... | collective-permute-start | bytes 98312 | tf_op jit(solution)/shard_map/ppermute | solution.py:52
  133.2 2.2 %copy-done.2 = bf16[32,256,256]{2,1,0:T(8,128)(2,1)S(1)} copy-done((bf16[32,256,256]{2,1,0:T(8,128)(2,1)S(1)}, bf16[32,256,256]{2,1,0:T(8,128)(2,1)}, u32[]{:S(2)}) %copy-start.2) | copy-done | bytes 4194328
  140.1 21.9 %all_to_all.5 = bf16[8,256,128]{2,1,0:T(8,128)(2,1)S(1)} all-to-all(bf16[8,256,128]{2,1,0:T(8,128)(2,1)S(1)} %shard_map.94), channel_id=1, replica_groups=mesh['chan'=4,'x'=4,'y'=4,'run'=2,'core'=2] {'run','chan'}, dimensions={0} | all-to-all | bytes 1048576 | tf_op jit(solution)/shard_map/all_to_all | solution.py:464
  (118 shorter events, 46.3 us)
Async XLA Ops:
  0.8 11.4 %collective-permute-start = (s32[144]{0:T(256)S(1)}, s32[144]{0:T(256)S(1)}, u32[]{:S(2)}, u32[]{:S(2)}) collective-permute-start(s32[144]{0:T(256)S(1)} %slice_add_fusion), channel_id=1, source_target_pairs={{0,1},{1,2},{2,3},{3,4},{4,5},{5,6},{6,7},{7,8},{8,9},{9,10},{10,1... | collective-permute-start | bytes 1736 | tf_op jit(solution)/shard_map/ppermute | solution.py:380
  3.9 20.8 %collective-permute-start.1 = (bf16[3,64,512]{2,1,0:T(8,128)(2,1)S(1)}, bf16[3,64,512]{2,1,0:T(8,128)(2,1)S(1)}, u32[]{:S(2)}, u32[]{:S(2)}) collective-permute-start(bf16[3,64,512]{2,1,0:T(8,128)(2,1)S(1)} %get-tuple-element.131), channel_id=1, source_target_pairs={{0,2},{1,3},{2,0},{3,1},{4,6},{5,7},{6,4},{7,5},{8,10},{9,11},{10,... | collective-permute-start | bytes 589832 | tf_op jit(solution)/shard_map/ppermute | solution.py:43
  24.7 14.3 %collective-permute-start.8 = (bf16[3,64,512]{2,1,0:T(8,128)(2,1)S(1)}, bf16[3,64,512]{2,1,0:T(8,128)(2,1)S(1)}, u32[]{:S(2)}, u32[]{:S(2)}) collective-permute-start(bf16[3,64,512]{2,1,0:T(8,128)(2,1)S(1)} %collective-permute-done.1), channel_id=1, source_target_pairs={{0,12},{1,13},{2,14},{3,15},{4,0},{5,1},{6,2},{7,3},{8,4},{9,5},{1... | collective-permute-start | bytes 589832 | tf_op jit(solution)/shard_map/ppermute | solution.py:39
  25.2 16.5 %collective-permute-start.9 = (bf16[3,64,512]{2,1,0:T(8,128)(2,1)S(1)}, bf16[3,64,512]{2,1,0:T(8,128)(2,1)S(1)}, u32[]{:S(2)}, u32[]{:S(2)}) collective-permute-start(bf16[3,64,512]{2,1,0:T(8,128)(2,1)S(1)} %collective-permute-done.1), channel_id=1, source_target_pairs={{0,8},{1,9},{2,10},{3,11},{4,12},{5,13},{6,14},{7,15},{8,0},{9,1},... | collective-permute-start | bytes 589832 | tf_op jit(solution)/shard_map/ppermute | solution.py:39
  27.8 14.8 %collective-permute-start.10 = (bf16[3,64,512]{2,1,0:T(8,128)(2,1)S(1)}, bf16[3,64,512]{2,1,0:T(8,128)(2,1)S(1)}, u32[]{:S(2)}, u32[]{:S(2)}) collective-permute-start(bf16[3,64,512]{2,1,0:T(8,128)(2,1)S(1)} %collective-permute-done.1), channel_id=1, source_target_pairs={{0,4},{1,5},{2,6},{3,7},{4,8},{5,9},{6,10},{7,11},{8,12},{9,13},{1... | collective-permute-start | bytes 589832 | tf_op jit(solution)/shard_map/ppermute | solution.py:39
  34.5 19.5 %collective-permute-start.3 = (bf16[512,512]{1,0:T(8,128)(2,1)S(1)}, bf16[512,512]{1,0:T(8,128)(2,1)S(1)}, u32[]{:S(2)}, u32[]{:S(2)}) collective-permute-start(bf16[512,512]{1,0:T(8,128)(2,1)S(1)} %constant_dynamic-update-slice_fusion.refs_0_), channel_id=1, source_target_pairs={{0,64},{1,65},{4,68},{5,69},{8,72},{9,73},{12,76},{13,77},{16,80},... | collective-permute-start | bytes 1572872 | tf_op jit(solution)/shard_map/ppermute | solution.py:68
  35.6 18.4 %collective-permute-start.4 = (bf16[512,512]{1,0:T(8,128)(2,1)S(1)}, bf16[512,512]{1,0:T(8,128)(2,1)S(1)}, u32[]{:S(2)}, u32[]{:S(2)}) collective-permute-start(bf16[512,512]{1,0:T(8,128)(2,1)S(1)} %constant_dynamic-update-slice_fusion.refs_0_), channel_id=1, source_target_pairs={{0,194},{1,195},{4,198},{5,199},{8,202},{9,203},{12,206},{13,207},... | collective-permute-start | bytes 1572872 | tf_op jit(solution)/shard_map/ppermute | solution.py:68
  39.0 11.2 %collective-permute-start.5 = (bf16[3,64,512]{2,1,0:T(8,128)(2,1)S(1)}, bf16[3,64,512]{2,1,0:T(8,128)(2,1)S(1)}, u32[]{:S(2)}, u32[]{:S(2)}) collective-permute-start(bf16[3,64,512]{2,1,0:T(8,128)(2,1)S(1)} %get-tuple-element.72), channel_id=1, source_target_pairs={{0,48},{1,49},{2,50},{3,51},{4,52},{5,53},{6,54},{7,55},{8,56},{9,... | collective-permute-start | bytes 589832 | tf_op jit(solution)/shard_map/ppermute | solution.py:35
  41.8 9.4 %collective-permute-start.6 = (bf16[3,64,512]{2,1,0:T(8,128)(2,1)S(1)}, bf16[3,64,512]{2,1,0:T(8,128)(2,1)S(1)}, u32[]{:S(2)}, u32[]{:S(2)}) collective-permute-start(bf16[3,64,512]{2,1,0:T(8,128)(2,1)S(1)} %get-tuple-element.72), channel_id=1, source_target_pairs={{0,32},{1,33},{2,34},{3,35},{4,36},{5,37},{6,38},{7,39},{8,40},{9,... | collective-permute-start | bytes 589832 | tf_op jit(solution)/shard_map/ppermute | solution.py:35
  42.6 11.3 %collective-permute-start.7 = (bf16[3,64,512]{2,1,0:T(8,128)(2,1)S(1)}, bf16[3,64,512]{2,1,0:T(8,128)(2,1)S(1)}, u32[]{:S(2)}, u32[]{:S(2)}) collective-permute-start(bf16[3,64,512]{2,1,0:T(8,128)(2,1)S(1)} %get-tuple-element.72), channel_id=1, source_target_pairs={{0,16},{1,17},{2,18},{3,19},{4,20},{5,21},{6,22},{7,23},{8,24},{9,... | collective-permute-start | bytes 589832 | tf_op jit(solution)/shard_map/ppermute | solution.py:35
  54.0 21.1 %collective-permute-start.13 = (bf16[4,3,64,512]{3,2,1,0:T(8,128)(2,1)S(1)}, bf16[4,3,64,512]{3,2,1,0:T(8,128)(2,1)S(1)}, u32[]{:S(2)}, u32[]{:S(2)}) collective-permute-start(bf16[4,3,64,512]{3,2,1,0:T(8,128)(2,1)S(1)} %pad_maximum_fusion.1.refs_2_), channel_id=1, source_target_pairs={{0,32},{1,33},{2,34},{3,35},{4,36},{5,37},{6,38},{7,39},{8,40},{9,... | collective-permute-start | bytes 2359304 | tf_op jit(solution)/shard_map/ppermute | solution.py:35
  54.9 20.2 %collective-permute-start.14 = (bf16[4,3,64,512]{3,2,1,0:T(8,128)(2,1)S(1)}, bf16[4,3,64,512]{3,2,1,0:T(8,128)(2,1)S(1)}, u32[]{:S(2)}, u32[]{:S(2)}) collective-permute-start(bf16[4,3,64,512]{3,2,1,0:T(8,128)(2,1)S(1)} %pad_maximum_fusion.refs_1_), channel_id=1, source_target_pairs={{0,12},{1,13},{2,14},{3,15},{4,0},{5,1},{6,2},{7,3},{8,4},{9,5},{1... | collective-permute-start | bytes 2359304 | tf_op jit(solution)/shard_map/ppermute | solution.py:39
  55.0 20.0 %collective-permute-start.15 = (bf16[4,3,64,512]{3,2,1,0:T(8,128)(2,1)S(1)}, bf16[4,3,64,512]{3,2,1,0:T(8,128)(2,1)S(1)}, u32[]{:S(2)}, u32[]{:S(2)}) collective-permute-start(bf16[4,3,64,512]{3,2,1,0:T(8,128)(2,1)S(1)} %pad_maximum_fusion.refs_1_), channel_id=1, source_target_pairs={{0,4},{1,5},{2,6},{3,7},{4,8},{5,9},{6,10},{7,11},{8,12},{9,13},{1... | collective-permute-start | bytes 2359304 | tf_op jit(solution)/shard_map/ppermute | solution.py:39
  56.9 14.2 %collective-permute-start.11 = (bf16[512,512]{1,0:T(8,128)(2,1)S(1)}, bf16[512,512]{1,0:T(8,128)(2,1)S(1)}, u32[]{:S(2)}, u32[]{:S(2)}) collective-permute-start(bf16[512,512]{1,0:T(8,128)(2,1)S(1)} %collective-permute-done.3.refs_0_), channel_id=1, source_target_pairs={{0,64},{1,65},{4,68},{5,69},{8,72},{9,73},{12,76},{13,77},{16,80},... | collective-permute-start | bytes 1572872 | tf_op jit(solution)/shard_map/ppermute | solution.py:68
  56.9 14.2 %collective-permute-start.12 = (bf16[512,512]{1,0:T(8,128)(2,1)S(1)}, bf16[512,512]{1,0:T(8,128)(2,1)S(1)}, u32[]{:S(2)}, u32[]{:S(2)}) collective-permute-start(bf16[512,512]{1,0:T(8,128)(2,1)S(1)} %collective-permute-done.4.refs_1_), channel_id=1, source_target_pairs={{0,194},{1,195},{4,198},{5,199},{8,202},{9,203},{12,206},{13,207},... | collective-permute-start | bytes 1572872 | tf_op jit(solution)/shard_map/ppermute | solution.py:68
  75.1 18.6 %collective-permute-start.18 = (bf16[4,3,64,512]{3,2,1,0:T(8,128)(2,1)S(1)}, bf16[4,3,64,512]{3,2,1,0:T(8,128)(2,1)S(1)}, u32[]{:S(2)}, u32[]{:S(2)}) collective-permute-start(bf16[4,3,64,512]{3,2,1,0:T(8,128)(2,1)S(1)} %pad_maximum_fusion.1.refs_2_), channel_id=1, source_target_pairs={{0,48},{1,49},{2,50},{3,51},{4,52},{5,53},{6,54},{7,55},{8,56},{9,... | collective-permute-start | bytes 2359304 | tf_op jit(solution)/shard_map/ppermute | solution.py:35
  75.1 19.9 %collective-permute-start.19 = (bf16[4,3,64,512]{3,2,1,0:T(8,128)(2,1)S(1)}, bf16[4,3,64,512]{3,2,1,0:T(8,128)(2,1)S(1)}, u32[]{:S(2)}, u32[]{:S(2)}) collective-permute-start(bf16[4,3,64,512]{3,2,1,0:T(8,128)(2,1)S(1)} %pad_maximum_fusion.1.refs_2_), channel_id=1, source_target_pairs={{0,16},{1,17},{2,18},{3,19},{4,20},{5,21},{6,22},{7,23},{8,24},{9,... | collective-permute-start | bytes 2359304 | tf_op jit(solution)/shard_map/ppermute | solution.py:35
  77.1 19.6 %collective-permute-start.20 = (bf16[4,3,64,512]{3,2,1,0:T(8,128)(2,1)S(1)}, bf16[4,3,64,512]{3,2,1,0:T(8,128)(2,1)S(1)}, u32[]{:S(2)}, u32[]{:S(2)}) collective-permute-start(bf16[4,3,64,512]{3,2,1,0:T(8,128)(2,1)S(1)} %pad_maximum_fusion.refs_1_), channel_id=1, source_target_pairs={{0,8},{1,9},{2,10},{3,11},{4,12},{5,13},{6,14},{7,15},{8,0},{9,1},... | collective-permute-start | bytes 2359304 | tf_op jit(solution)/shard_map/ppermute | solution.py:39
  78.6 13.5 %collective-permute-start.16 = (bf16[512,512]{1,0:T(8,128)(2,1)S(1)}, bf16[512,512]{1,0:T(8,128)(2,1)S(1)}, u32[]{:S(2)}, u32[]{:S(2)}) collective-permute-start(bf16[512,512]{1,0:T(8,128)(2,1)S(1)} %collective-permute-done.11.refs_0_), channel_id=1, source_target_pairs={{0,64},{1,65},{4,68},{5,69},{8,72},{9,73},{12,76},{13,77},{16,80},... | collective-permute-start | bytes 1572872 | tf_op jit(solution)/shard_map/ppermute | solution.py:68
  78.6 13.5 %collective-permute-start.17 = (bf16[512,512]{1,0:T(8,128)(2,1)S(1)}, bf16[512,512]{1,0:T(8,128)(2,1)S(1)}, u32[]{:S(2)}, u32[]{:S(2)}) collective-permute-start(bf16[512,512]{1,0:T(8,128)(2,1)S(1)} %collective-permute-done.12.refs_1_), channel_id=1, source_target_pairs={{0,194},{1,195},{4,198},{5,199},{8,202},{9,203},{12,206},{13,207},... | collective-permute-start | bytes 1572872 | tf_op jit(solution)/shard_map/ppermute | solution.py:68
  97.4 7.7 %collective-permute-start.21 = (bf16[256,512]{1,0:T(8,128)(2,1)S(1)}, bf16[256,512]{1,0:T(8,128)(2,1)S(1)}, u32[]{:S(2)}, u32[]{:S(2)}) collective-permute-start(bf16[256,512]{1,0:T(8,128)(2,1)S(1)} %get-tuple-element.101), channel_id=1, source_target_pairs={{0,64},{1,65},{4,68},{5,69},{8,72},{9,73},{12,76},{13,77},{16,80},... | collective-permute-start | bytes 786440 | tf_op jit(solution)/shard_map/ppermute | solution.py:68
  97.5 7.6 %collective-permute-start.22 = (bf16[256,512]{1,0:T(8,128)(2,1)S(1)}, bf16[256,512]{1,0:T(8,128)(2,1)S(1)}, u32[]{:S(2)}, u32[]{:S(2)}) collective-permute-start(bf16[256,512]{1,0:T(8,128)(2,1)S(1)} %get-tuple-element.102), channel_id=1, source_target_pairs={{0,194},{1,195},{4,198},{5,199},{8,202},{9,203},{12,206},{13,207},... | collective-permute-start | bytes 786440 | tf_op jit(solution)/shard_map/ppermute | solution.py:68
  125.1 13.4 %collective-permute-start.28 = (f32[16,512]{1,0:T(8,128)S(1)}, f32[16,512]{1,0:T(8,128)S(1)}, u32[]{:S(2)}, u32[]{:S(2)}) collective-permute-start(f32[16,512]{1,0:T(8,128)S(1)} %multiply_add_fusion.2), channel_id=1, source_target_pairs={{0,16},{1,17},{2,18},{3,19},{4,20},{5,21},{6,22},{7,23},{8,24},{9,... | collective-permute-start | bytes 98312 | tf_op jit(solution)/shard_map/ppermute | solution.py:52
  127.9 10.5 %collective-permute-start.29 = (f32[16,512]{1,0:T(8,128)S(1)}, f32[16,512]{1,0:T(8,128)S(1)}, u32[]{:S(2)}, u32[]{:S(2)}) collective-permute-start(f32[16,512]{1,0:T(8,128)S(1)} %multiply_add_fusion.2), channel_id=1, source_target_pairs={{0,32},{1,33},{2,34},{3,35},{4,36},{5,37},{6,38},{7,39},{8,40},{9,... | collective-permute-start | bytes 98312 | tf_op jit(solution)/shard_map/ppermute | solution.py:52
  (22 other events, 157.2 us)
where the time goes:
time: 163 us
  starting transfers between devices  51.4 us (32%)
  waiting for transfers between devices  43.2 us (27%)
  Pallas kernels  29.9 us (18%)
  blocking collectives  21.9 us (13%)
  local copies, waits for them, and re-layouts  11 us (7%)
  other arithmetic  4.67 us (3%)
    all_to_all x1, blocking collectives, shards(): terms = lax.all_to_all(terms, ('run', 'chan'), 0, 0, tiled=True)  21.9 us
    ppermute x8, waiting for transfers between devices, to_z(): return lax.ppermute(v, ('chan',) + SEQ, pairs)  19.7 us
    ppermute x6, waiting for transfers between devices, from_x(): lax.ppermute(v, SEQ, seq_pairs(lambda x, y, h, c: ((x - j) % NX, y, h, c)))  17.1 us
    ppermute x8, starting transfers between devices, to_z(): return lax.ppermute(v, ('chan',) + SEQ, pairs)  13.6 us
    ppermute x9, starting transfers between devices, from_y(): lax.ppermute(v, SEQ, seq_pairs(lambda x, y, h, c: (x, (y - j) % NY, h, c)))  12.5 us
    unnamed x31, local copies, waits for them, and re-layouts  8.8 us
    pallas_call x1, Pallas kernels, activations(): pl.pallas_call(act_kernel, grid=(4,), out_shape=(jax.ShapeDtypeStruct((25...  8.74 us
    pallas_call x2, Pallas kernels, li_terms(): pl.pallas_call(functools.partial(li_kernel, which), out_shape=jax.ShapeDt...  8.47 us
  transfers between devices with their start and end apart: 31, of which 13 were waited for; matrix products, arithmetic and copies ran while one was open for 3% of the time, Pallas kernels for 14%

commit v1 on v0

--- a/solution.py
+++ b/solution.py
@@ -47,9 +47,12 @@
     return lax.ppermute(v, SEQ, seq_pairs(lambda x, y, h, c: (x, y, h, 1 - c)))
 
 
-def from_x_before(v, j):
-    pairs = [(seq_of(x, y, h, c), seq_of(x + j, y, h, c)) for x, y, h, c in COORDS if x + j < NX]
-    return lax.ppermute(v, SEQ, pairs)
+def y_swap(step):
+    return seq_pairs(lambda x, y, h, c: (x, y ^ step, h, c))
+
+
+def x_swap(step):
+    return seq_pairs(lambda x, y, h, c: (x ^ step, y, h, c))
 
 
 def to_z(v, d):
@@ -151,25 +154,6 @@
         compiler_params=pltpu.CompilerParams(vmem_limit_bytes=12 * 2**20),
         cost_estimate=pl.CostEstimate(flops=4 * 10**9, bytes_accessed=8 * 10**6, transcendentals=0),
     )(where, ids, emb, sf, mr_rows)
-
-
-def toeplitz_kernel(h_ref, out_ref):
-    for g in range(8):
-        base = jnp.broadcast_to(h_ref[g : g + 1, :], (256, 512))
-        out_ref[g] = pltpu.roll(base, 0, 1, stride=1, stride_axis=0)[:, :256].astype(BF16)
-
-
-def toeplitz(base_rows):
-    groups = base_rows.shape[0]
-    return pl.pallas_call(
-        toeplitz_kernel,
-        grid=(groups // 8,),
-        out_shape=jax.ShapeDtypeStruct((groups, 256, 256), BF16),
-        in_specs=[pl.BlockSpec((8, 512), lambda i: (i, 0))],
-        out_specs=pl.BlockSpec((8, 256, 256), lambda i: (i, 0, 0)),
-        compiler_params=pltpu.CompilerParams(vmem_limit_bytes=12 * 2**20),
-        cost_estimate=pl.CostEstimate(flops=10**7, bytes_accessed=4 * 10**6, transcendentals=0),
-    )(base_rows)
 
 
 def block_place(where, d):
@@ -301,33 +285,34 @@
     )(own, got, fade)
 
 
-def inner_kernel(x_ref, t_ref, out_ref):
+def inner_kernel(x_ref, h_ref, out_ref):
     both = jnp.concatenate([x_ref[:256, :], x_ref[256:, :]], axis=1)
     group = (lax.broadcasted_iota(jnp.int32, (256, 256), 1) // GSIZE) % 8
-    total = jnp.dot(t_ref[0], both, preferred_element_type=F32)
-    for g in range(1, 8):
-        total = jnp.where(
-            group == g, jnp.dot(t_ref[g], both, preferred_element_type=F32), total
-        )
+    total = None
+    for g in range(8):
+        base = jnp.broadcast_to(h_ref[g : g + 1, :], (256, 512))
+        block = pltpu.roll(base, 0, 1, stride=1, stride_axis=0)[:, :256].astype(BF16)
+        part = jnp.dot(block, both, preferred_element_type=F32)
+        total = part if g == 0 else jnp.where(group == g, part, total)
     out_ref[:256, :] = total[:, :128]
     out_ref[256:, :] = total[:, 128:]
 
 
-def inner(mixed, blocks):
+def inner(mixed, base_rows):
     return pl.pallas_call(
         inner_kernel,
         grid=(4,),
         out_shape=jax.ShapeDtypeStruct((512, 512), F32),
         in_specs=[
             pl.BlockSpec((512, 128), lambda i: (0, i)),
-            pl.BlockSpec((8, 256, 256), lambda i: (i, 0, 0)),
+            pl.BlockSpec((8, 512), lambda i: (i, 0)),
         ],
         out_specs=pl.BlockSpec((512, 128), lambda i: (0, i)),
         compiler_params=pltpu.CompilerParams(vmem_limit_bytes=12 * 2**20),
         cost_estimate=pl.CostEstimate(
-            flops=43 * 10**8, bytes_accessed=6 * 10**6, transcendentals=0
+            flops=43 * 10**8, bytes_accessed=2 * 10**6, transcendentals=0
         ),
-    )(mixed, blocks)
+    )(mixed, base_rows)
 
 
 def logits_kernel(start_ref, inner_ref, q_ref, log_ref, coef_ref, proj_ref, out_ref, li_out):
@@ -389,8 +374,11 @@
     taps = jnp.transpose(short_filter, (1, 0, 2))
     filt = lax.dynamic_slice_in_dim(mr_filter, chan * 64, 64, 0).astype(F32)
     mr_rows = jnp.pad(filt[:, ::-1], ((0, 0), (1, 127)))
+    a_x = [mine] + [from_x(mine, j) for j in (1, 2, 3)]
+    ext_ids, rows_b, a_x = tie((ext_ids, rows_b, a_x))
+    a_x = jnp.stack(a_x)
+    b_y = jnp.stack([rows_b] + [from_y(rows_b, k) for k in (1, 2, 3)])
     keep, send = activations(where, ext_ids, emb, taps, mr_rows)
-    keep, send, mine, rows_b = tie((keep, send, mine, rows_b))
     rate, residue, out_proj, keep = tie((rate, residue, out_proj, keep))
     first = chan * 64 + h * 32
     log_all = -lax.dynamic_slice_in_dim(rate, first, 32, 0) / total_len
@@ -398,7 +386,6 @@
     lag = (512 - jnp.arange(512)) % 512
     power = jnp.exp(lag.astype(F32)[None, None, :] * log_all[:, :, None])
     base_rows = jnp.where(lag[None, :] < 256, jnp.sum(coef[:, :, None] * power, axis=1), 0.0)
-    blocks = toeplitz(base_rows)
     log_row = log_all.reshape(1, 512)
     coef_row = coef.reshape(1, 512)
     fade = jnp.exp(log_all.reshape(512, 1) * (255 - jnp.arange(256)).astype(F32)[None, :])
@@ -408,30 +395,34 @@
         return jnp.where(keep, jnp.exp(steps * log_ch), 0.0)
 
     rows_of = 4.0 * ids.shape[0]
-    one, row_step = decay(256.0), decay(4096.0)
-    to_row = decay(rows_of * y.astype(F32))
-    before = [decay(rows_of * (d - 1), d <= y) for d in (1, 2, 3)]
-    within = [decay(rows_of * (3 - (y - d) % 4).astype(F32)) for d in range(4)]
+    one = decay(256.0)
+    spans, offsets = [], []
+    for size, upper, offset in (
+        (1, y % 2, 0 * y),
+        (2, y // 2, y % 2),
+        (4, x % 2, y),
+        (8, x // 2, y + 4 * (x % 2)),
+    ):
+        spans.append(decay(rows_of * size))
+        offsets.append(decay(rows_of * offset.astype(F32), upper == 1))
     proj = lax.dynamic_slice_in_dim(out_proj, h * 512, 512, 0)
     own = jnp.concatenate([keep, from_core(send)], axis=0)
 
-    a_x = jnp.stack([mine] + [from_x(mine, j) for j in (1, 2, 3)])
-    b_y = jnp.stack([rows_b] + [from_y(rows_b, k) for k in (1, 2, 3)])
+    full = gather(where, None, [(0, 0, 2, own)], [(True, 0, a_x), (False, 0, b_y)])
     up1, down1 = to_z(own, 1), to_z(own, -1)
-    params = (fade, one, row_step, to_row, before, within, log_row, coef_row, proj, blocks)
-    up1, down1, a_x, b_y, params = tie((up1, down1, a_x, b_y, params))
-    fade, one, row_step, to_row, before, within, log_row, coef_row, proj, blocks = params
-    full = gather(where, None, [(0, 0, 2, own)], [(True, 0, a_x), (False, 0, b_y)])
+    x2, y1, y3 = from_x(b_y, 2), from_y(a_x, 1), from_y(a_x, 3)
+    params = (fade, one, spans, offsets, log_row, coef_row, proj, base_rows)
+    up1, down1, params = tie((up1, down1, params))
+    fade, one, spans, offsets, log_row, coef_row, proj, base_rows = params
+    full = gather(where, full, [(-1, 0, 2, up1), (1, 0, 2, down1)], [])
     up2, down2 = to_z(up1, 1), to_z(down1, -1)
-    x2, y1, y3 = from_x(b_y, 2), from_y(a_x, 1), from_y(a_x, 3)
-    full = gather(where, full, [(-1, 0, 2, up1), (1, 0, 2, down1)], [])
-    up2, down2, x2, y1, y3, a_x, b_y, full = tie((up2, down2, x2, y1, y3, a_x, b_y, full))
-    up3, down3 = to_z(up2, 1), to_z(down2, -1)
+    x2, y1, y3, a_x, b_y = tie((x2, y1, y3, a_x, b_y))
     x1, x3, y2 = from_x(b_y, 1), from_x(b_y, 3), from_y(a_x, 2)
     full = gather(
         where, full, [(-2, 0, 2, up2), (2, 0, 2, down2)], [(False, 2, x2), (True, 1, y1), (True, 3, y3)]
     )
-    up3, down3, x1, x3, y2, full = tie((up3, down3, x1, x3, y2, full))
+    up2, down2, x2 = tie((up2, down2, x2))
+    up3, down3 = to_z(up2, 1), to_z(down2, -1)
     *full, top, bottom = gather(where, full, [(-3, 0, 2, up3), (3, 0, 2, down3)], [], True)
     up4, down4 = to_z(top, 1), to_z(bottom, -1)
     full = gather(where, full, [], [(False, 1, x1), (False, 3, x3), (True, 2, y2)])
@@ -441,20 +432,22 @@
     got = from_core(give)
     have = li_terms(0, *full)
     q2, mixed, states = block_states(have, got, fade)
-    inside = inner(mixed, blocks)
+    inside = inner(mixed, base_rows)
 
     other = from_core(states)
     early = jnp.where(c == 0, states, other)
     late = jnp.where(c == 0, other, states)
     s0, s1, s2, s3 = early[0], late[0], early[1], late[1]
     total = s3 + one * (s2 + one * (s1 + one * s0))
-    along_y = [total] + [from_y(total, k) for k in (3, 2, 1)]
-    row_total = sum(within[d] * along_y[d] for d in range(4))
-    before_y = sum(before[d - 1] * along_y[d] for d in (1, 2, 3))
-    before_x = from_x_before(row_total, 1) + row_step * (
-        from_x_before(row_total, 2) + row_step * from_x_before(row_total, 3)
-    )
-    at = before_y + to_row * before_x
+    at = jnp.zeros_like(total)
+    for n, (bit, swap) in enumerate(
+        ((y % 2, y_swap(1)), (y // 2, y_swap(2)), (x % 2, x_swap(1)), (x // 2, x_swap(2)))
+    ):
+        there = lax.ppermute(total, SEQ, swap)
+        at = at + offsets[n] * there
+        total = jnp.where(
+            bit == 1, spans[n] * there + total, spans[n] * total + there
+        )
     at1 = s0 + one * at
     at2 = s1 + one * at1
     at3 = s2 + one * at2

time: 163 us -> 148 us (0.908)
  blocking collectives: 21.9 us -> 16.4 us
  local copies, waits for them, and re-layouts: 11 us -> 5.85 us
  waiting for transfers between devices: 43.2 us -> 38.4 us
  starting transfers between devices: 51.4 us -> 48.7 us
  other arithmetic: 4.67 us -> 6.62 us
    ppermute x8, waiting for transfers between devices: 19.7 us -> 6.97 us  [to_z(): return lax.ppermute(v, ('chan',) + SEQ, pairs)]
    ppermute x6, waiting for transfers between devices: 17.1 us -> 5.43 us  [from_x(): lax.ppermute(v, SEQ, seq_pairs(lambda x, y, h, c: ((x - j) % NX, y, h, c)))]
    ppermute x3 -> x4, waiting for transfers between devices: 0.01 us -> 9.81 us  [shards(): there = lax.ppermute(total, SEQ, swap)]
    ppermute x1, waiting for transfers between devices: 0.01 us -> 6.73 us  [shards(): lax.ppermute(ids[ids.shape[0] - HALO:] + 1, SEQ, [(i, i + 1) for i in ran...]
    unnamed x31 -> x25, local copies, waits for them, and re-layouts: 8.8 us -> 2.84 us
    all_to_all x1, blocking collectives: 21.9 us -> 16.4 us  [shards(): terms = lax.all_to_all(terms, ('run', 'chan'), 0, 0, tiled=True)]
    ppermute x9 -> x6, starting transfers between devices: 12.5 us -> 9.4 us  [from_y(): lax.ppermute(v, SEQ, seq_pairs(lambda x, y, h, c: (x, (y - j) % NY, h, c)))]
    ppermute x9 -> x6, waiting for transfers between devices: 5.51 us -> 8.53 us  [from_y(): lax.ppermute(v, SEQ, seq_pairs(lambda x, y, h, c: (x, (y - j) % NY, h, c)))]
  transfers between devices with their start and end apart: 31 -> 29, of which waited for: 13 -> 13; matrix products, arithmetic and copies ran while one was open for 3% -> 5% of each run, Pallas kernels for 14% -> 16%
where the time goes in v1:
time: 148 us; the launch traced here: 147 us
  starting transfers between devices  48.7 us (33%)
  waiting for transfers between devices  38.4 us (26%)
  Pallas kernels  30.4 us (21%)
  blocking collectives  16.4 us (11%)
  other arithmetic  6.62 us (4%)
  local copies, waits for them, and re-layouts  5.85 us (4%)
    all_to_all x1, blocking collectives, shards(): terms = lax.all_to_all(terms, ('run', 'chan'), 0, 0, tiled=True)  16.4 us
    ppermute x8, starting transfers between devices, to_z(): return lax.ppermute(v, ('chan',) + SEQ, pairs)  13.2 us
    ppermute x4, waiting for transfers between devices, shards(): there = lax.ppermute(total, SEQ, swap)  9.81 us
    ppermute x6, starting transfers between devices, from_y(): lax.ppermute(v, SEQ, seq_pairs(lambda x, y, h, c: (x, (y - j) % NY, h, c)))  9.4 us
    ppermute x6, starting transfers between devices, from_x(): lax.ppermute(v, SEQ, seq_pairs(lambda x, y, h, c: ((x - j) % NX, y, h, c)))  9.17 us
    pallas_call x1, Pallas kernels, activations(): pl.pallas_call(act_kernel, grid=(4,), out_shape=(jax.ShapeDtypeStruct((25...  8.74 us
    pallas_call x6, Pallas kernels, gather(): pl.pallas_call(functools.partial(gather_kernel, steps, plan, halves), out...  8.73 us
    ppermute x6, waiting for transfers between devices, from_y(): lax.ppermute(v, SEQ, seq_pairs(lambda x, y, h, c: (x, (y - j) % NY, h, c)))  8.53 us
  transfers between devices with their start and end apart: 29, of which 13 were waited for; matrix products, arithmetic and copies ran while one was open for 5% of the time, Pallas kernels for 16%

profile of v1, /device:TPU:8, one launch (start us, length us, event | category | flops | bytes accessed | tf_op | source)
XLA Modules:
  0.0 146.9 jit_solution(349603783862649189)
XLA Ops:
  1.1 2.8 %collective-permute-start.2 = (bf16[3,64,512]{2,1,0:T(8,128)(2,1)S(1)}, bf16[3,64,512]{2,1,0:T(8,128)(2,1)S(1)}, u32[]{:S(2)}, u32[]{:S(2)}) collective-permute-start(bf16[3,64,512]{2,1,0:T(8,128)(2,1)S(1)} %get-tuple-element.67), channel_id=1, source_target_pairs={{0,48},{1,49},{2,50},{3,51},{4,52},{5,53},{6,54},{7,55},{8,56},{9,... | collective-permute-start | bytes 589832 | tf_op jit(solution)/shard_map/ppermute | solution.py:35
  5.7 7.2 %collective-permute-start.1 = (bf16[3,64,512]{2,1,0:T(8,128)(2,1)S(1)}, bf16[3,64,512]{2,1,0:T(8,128)(2,1)S(1)}, u32[]{:S(2)}, u32[]{:S(2)}) collective-permute-start(bf16[3,64,512]{2,1,0:T(8,128)(2,1)S(1)} %get-tuple-element.110), channel_id=1, source_target_pairs={{0,2},{1,3},{2,0},{3,1},{4,6},{5,7},{6,4},{7,5},{8,10},{9,11},{10,... | collective-permute-start | bytes 589832 | tf_op jit(solution)/shard_map/ppermute | solution.py:43
  16.7 6.7 %collective-permute-done = s32[144]{0:T(256)S(1)} collective-permute-done((s32[144]{0:T(256)S(1)}, s32[144]{0:T(256)S(1)}, u32[]{:S(2)}, u32[]{:S(2)}) %collective-permute-start) | collective-permute-done | bytes 608 | tf_op jit(solution)/shard_map/ppermute | solution.py:365
  24.3 3.1 %collective-permute-start.11 = (bf16[3,64,512]{2,1,0:T(8,128)(2,1)S(1)}, bf16[3,64,512]{2,1,0:T(8,128)(2,1)}, u32[]{:S(2)}, u32[]{:S(2)}) collective-permute-start(bf16[3,64,512]{2,1,0:T(8,128)(2,1)S(1)} %collective-permute-done.1), channel_id=1, source_target_pairs={{0,8},{1,9},{2,10},{3,11},{4,12},{5,13},{6,14},{7,15},{8,0},{9,1},... | collective-permute-start | bytes 589832 | tf_op jit(solution)/shard_map/ppermute | solution.py:39
  32.1 8.7 %shard_map.82 = (bf16[256,512]{1,0:T(8,128)(2,1)S(1)}, bf16[256,512]{1,0:T(8,128)(2,1)S(1)}) custom-call(s32[5]{0:T(128)S(1)} %stack.62.where, s32[400,1]{1,0:T(8,128)S(1)} %copy.29.ids_ref, bf16[3,512,1024]{2,1,0:T(8,128)(2,1)S(1)} %bitcast.51, f32[3,7,1024]{2,1,0:T(8,128)S(1)} %bitcast.52, f32[64,256]{1,0:T(8,128)S(1)} %pad.4.mr_ref), custom_call_target="tpu_custom_call" | custom-call | flops 4000000000 | bytes 8000000 | tf_op jit(solution)/shard_map/pallas_call | solution.py:136
  43.7 2.3 %collective-permute-start.7 = (bf16[512,512]{1,0:T(8,128)(2,1)S(1)}, bf16[512,512]{1,0:T(8,128)(2,1)}, u32[]{:S(2)}, u32[]{:S(2)}) collective-permute-start(bf16[512,512]{1,0:T(8,128)(2,1)S(1)} %constant_dynamic-update-slice_fusion.refs_0_), channel_id=1, source_target_pairs={{0,194},{1,195},{4,198},{5,199},{8,202},{9,203},{12,206},{13,207},... | collective-permute-start | bytes 1572872 | tf_op jit(solution)/shard_map/ppermute | solution.py:71
  53.7 4.7 %collective-permute-done.6.refs_0_ = bf16[512,512]{1,0:T(8,128)(2,1)} collective-permute-done((bf16[512,512]{1,0:T(8,128)(2,1)S(1)}, bf16[512,512]{1,0:T(8,128)(2,1)}, u32[]{:S(2)}, u32[]{:S(2)}) %collective-permute-start.6) | collective-permute-done | bytes 524320 | tf_op jit(solution)/shard_map/ppermute | solution.py:71
  58.8 2.8 %collective-permute-start.9 = (bf16[512,512]{1,0:T(8,128)(2,1)}, bf16[512,512]{1,0:T(8,128)(2,1)S(1)}, u32[]{:S(2)}, u32[]{:S(2)}) collective-permute-start(bf16[512,512]{1,0:T(8,128)(2,1)} %collective-permute-done.7.refs_1_), channel_id=1, source_target_pairs={{0,194},{1,195},{4,198},{5,199},{8,202},{9,203},{12,206},{13,207},... | collective-permute-start | bytes 1572872 | tf_op jit(solution)/shard_map/ppermute | solution.py:71
  61.6 5.0 %collective-permute-done.14.refs_3_ = bf16[4,3,64,512]{3,2,1,0:T(8,128)(2,1)} collective-permute-done((bf16[4,3,64,512]{3,2,1,0:T(8,128)(2,1)S(1)}, bf16[4,3,64,512]{3,2,1,0:T(8,128)(2,1)}, u32[]{:S(2)}, u32[]{:S(2)}) %collective-permute-start.14) | collective-permute-done | bytes 786464 | tf_op jit(solution)/shard_map/ppermute | solution.py:39
  67.0 4.1 %collective-permute-done.13.refs_2_ = bf16[4,3,64,512]{3,2,1,0:T(8,128)(2,1)} collective-permute-done((bf16[4,3,64,512]{3,2,1,0:T(8,128)(2,1)S(1)}, bf16[4,3,64,512]{3,2,1,0:T(8,128)(2,1)}, u32[]{:S(2)}, u32[]{:S(2)}) %collective-permute-start.13) | collective-permute-done | bytes 786464 | tf_op jit(solution)/shard_map/ppermute | solution.py:35
  71.0 2.5 %collective-permute-start.20 = (bf16[4,3,64,512]{3,2,1,0:T(8,128)(2,1)S(1)}, bf16[4,3,64,512]{3,2,1,0:T(8,128)(2,1)S(1)}, u32[]{:S(2)}, u32[]{:S(2)}) collective-permute-start(bf16[4,3,64,512]{3,2,1,0:T(8,128)(2,1)S(1)} %pad_maximum_fusion.refs_2_), channel_id=1, source_target_pairs={{0,48},{1,49},{2,50},{3,51},{4,52},{5,53},{6,54},{7,55},{8,56},{9,... | collective-permute-start | bytes 2359304 | tf_op jit(solution)/shard_map/ppermute | solution.py:35
  73.7 3.2 %collective-permute-start.17 = (bf16[512,512]{1,0:T(8,128)(2,1)S(1)}, bf16[512,512]{1,0:T(8,128)(2,1)S(1)}, u32[]{:S(2)}, u32[]{:S(2)}) collective-permute-start(bf16[512,512]{1,0:T(8,128)(2,1)S(1)} %collective-permute-done.9.refs_1_), channel_id=1, source_target_pairs={{0,194},{1,195},{4,198},{5,199},{8,202},{9,203},{12,206},{13,207},... | collective-permute-start | bytes 1572872 | tf_op jit(solution)/shard_map/ppermute | solution.py:71
  76.9 2.3 %collective-permute-start.22 = (bf16[4,3,64,512]{3,2,1,0:T(8,128)(2,1)S(1)}, bf16[4,3,64,512]{3,2,1,0:T(8,128)(2,1)S(1)}, u32[]{:S(2)}, u32[]{:S(2)}) collective-permute-start(bf16[4,3,64,512]{3,2,1,0:T(8,128)(2,1)S(1)} %pad_maximum_fusion.1.refs_1_), channel_id=1, source_target_pairs={{0,8},{1,9},{2,10},{3,11},{4,12},{5,13},{6,14},{7,15},{8,0},{9,1},... | collective-permute-start | bytes 2359304 | tf_op jit(solution)/shard_map/ppermute | solution.py:39
  82.0 2.9 %shard_map.85 = (bf16[2,512,2048]{2,1,0:T(8,128)(2,1)S(1)}, bf16[3,2048,512]{2,1,0:T(8,128)(2,1)S(1)}) custom-call(s32[5]{0:T(128)S(1)} %stack.62.where, bf16[512,512]{1,0:T(8,128)(2,1)S(1)} %collective-permute-done.8.refs_0_, bf16[512,512]{1,0:T(8,128)(2,1)S(1)} %collective-permute-done.9.refs_1_, ...), custom_call_target="tpu_custom_call", output_to_operand_aliasing={{0}: (6, {}), {1}: (7, {})} | custom-call | flops 1000000 | bytes 6000000 | tf_op jit(solution)/shard_map/pallas_call | solution.py:210
  84.9 2.3 %collective-permute-done.16.refs_0_ = bf16[512,512]{1,0:T(8,128)(2,1)S(1)} collective-permute-done((bf16[512,512]{1,0:T(8,128)(2,1)S(1)}, bf16[512,512]{1,0:T(8,128)(2,1)S(1)}, u32[]{:S(2)}, u32[]{:S(2)}) %collective-permute-start.16) | collective-permute-done | bytes 524320 | tf_op jit(solution)/shard_map/ppermute | solution.py:71
  88.0 3.2 %collective-permute-start.19 = (bf16[256,512]{1,0:T(8,128)(2,1)S(1)}, bf16[256,512]{1,0:T(8,128)(2,1)S(1)}, u32[]{:S(2)}, u32[]{:S(2)}) collective-permute-start(bf16[256,512]{1,0:T(8,128)(2,1)S(1)} %get-tuple-element.83), channel_id=1, source_target_pairs={{0,194},{1,195},{4,198},{5,199},{8,202},{9,203},{12,206},{13,207},... | collective-permute-start | bytes 786440 | tf_op jit(solution)/shard_map/ppermute | solution.py:71
  92.6 3.2 %collective-permute-done.22.refs_2_ = bf16[4,3,64,512]{3,2,1,0:T(8,128)(2,1)S(1)} collective-permute-done((bf16[4,3,64,512]{3,2,1,0:T(8,128)(2,1)S(1)}, bf16[4,3,64,512]{3,2,1,0:T(8,128)(2,1)S(1)}, u32[]{:S(2)}, u32[]{:S(2)}) %collective-permute-start.22) | collective-permute-done | bytes 786464 | tf_op jit(solution)/shard_map/ppermute | solution.py:39
  98.1 4.2 %shard_map.90 = bf16[3,512,512]{2,1,0:T(8,128)(2,1)S(1)} custom-call(bf16[2,512,2048]{2,1,0:T(8,128)(2,1)S(1)} %get-tuple-element.90.a_ref, bf16[3,2048,512]{2,1,0:T(8,128)(2,1)S(1)} %get-tuple-element.91.w_ref), custom_call_target="tpu_custom_call" | custom-call | flops 3300000000 | bytes 10000000 | tf_op jit(solution)/shard_map/pallas_call | solution.py:237
  102.5 4.2 %shard_map.89.own_ref = f32[3,512,512]{2,1,0:T(8,128)S(1)} custom-call(bf16[2,512,2048]{2,1,0:T(8,128)(2,1)S(1)} %get-tuple-element.90.a_ref, bf16[3,2048,512]{2,1,0:T(8,128)(2,1)S(1)} %get-tuple-element.91.w_ref), custom_call_target="tpu_custom_call" | custom-call | flops 3300000000 | bytes 10000000 | tf_op jit(solution)/shard_map/pallas_call | solution.py:237
  109.7 3.4 %collective-permute-done.25 = f32[16,512]{1,0:T(8,128)S(1)} collective-permute-done((f32[16,512]{1,0:T(8,128)S(1)}, f32[16,512]{1,0:T(8,128)S(1)}, u32[]{:S(2)}, u32[]{:S(2)}) %collective-permute-start.25) | collective-permute-done | bytes 32800 | tf_op jit(solution)/shard_map/ppermute | solution.py:446
  115.2 3.4 %collective-permute-done.26 = f32[16,512]{1,0:T(8,128)S(1)} collective-permute-done((f32[16,512]{1,0:T(8,128)S(1)}, f32[16,512]{1,0:T(8,128)S(1)}, u32[]{:S(2)}, u32[]{:S(2)}) %collective-permute-start.26) | collective-permute-done | bytes 32800 | tf_op jit(solution)/shard_map/ppermute | solution.py:446
  122.7 2.3 %collective-permute-start.28 = (f32[16,512]{1,0:T(8,128)S(1)}, f32[16,512]{1,0:T(8,128)S(1)}, u32[]{:S(2)}, u32[]{:S(2)}) collective-permute-start(f32[16,512]{1,0:T(8,128)S(1)} %add_select_fusion), channel_id=1, source_target_pairs={{0,32},{1,33},{2,34},{3,35},{4,36},{5,37},{6,38},{7,39},{8,40},{9,... | collective-permute-start | bytes 98312 | tf_op jit(solution)/shard_map/ppermute | solution.py:446
  125.0 2.3 %shard_map.92.inner_ref = f32[512,512]{1,0:T(8,128)S(1)} custom-call(bf16[512,512]{1,0:T(8,128)(2,1)S(1)} %get-tuple-element.101.x_ref, f32[32,512]{1,0:T(8,128)S(1)} %broadcast_select_fusion.h_ref), custom_call_target="tpu_custom_call" | custom-call | flops 4300000256 | bytes 2000000 | tf_op jit(solution)/shard_map/pallas_call | solution.py:302
  129.8 16.4 %all_to_all.5 = bf16[8,256,128]{2,1,0:T(8,128)(2,1)S(1)} all-to-all(bf16[8,256,128]{2,1,0:T(8,128)(2,1)S(1)} %shard_map.93), channel_id=1, replica_groups=mesh['chan'=4,'x'=4,'y'=4,'run'=2,'core'=2] {'run','chan'}, dimensions={0} | all-to-all | bytes 1048576 | tf_op jit(solution)/shard_map/all_to_all | solution.py:457
  (109 shorter events, 43.0 us)
Async XLA Ops:
  1.1 23.0 %collective-permute-start.2 = (bf16[3,64,512]{2,1,0:T(8,128)(2,1)S(1)}, bf16[3,64,512]{2,1,0:T(8,128)(2,1)S(1)}, u32[]{:S(2)}, u32[]{:S(2)}) collective-permute-start(bf16[3,64,512]{2,1,0:T(8,128)(2,1)S(1)} %get-tuple-element.67), channel_id=1, source_target_pairs={{0,48},{1,49},{2,50},{3,51},{4,52},{5,53},{6,54},{7,55},{8,56},{9,... | collective-permute-start | bytes 589832 | tf_op jit(solution)/shard_map/ppermute | solution.py:35
  4.0 20.2 %collective-permute-start.3 = (bf16[3,64,512]{2,1,0:T(8,128)(2,1)S(1)}, bf16[3,64,512]{2,1,0:T(8,128)(2,1)S(1)}, u32[]{:S(2)}, u32[]{:S(2)}) collective-permute-start(bf16[3,64,512]{2,1,0:T(8,128)(2,1)S(1)} %get-tuple-element.67), channel_id=1, source_target_pairs={{0,32},{1,33},{2,34},{3,35},{4,36},{5,37},{6,38},{7,39},{8,40},{9,... | collective-permute-start | bytes 589832 | tf_op jit(solution)/shard_map/ppermute | solution.py:35
  4.8 19.4 %collective-permute-start.4 = (bf16[3,64,512]{2,1,0:T(8,128)(2,1)S(1)}, bf16[3,64,512]{2,1,0:T(8,128)(2,1)S(1)}, u32[]{:S(2)}, u32[]{:S(2)}) collective-permute-start(bf16[3,64,512]{2,1,0:T(8,128)(2,1)S(1)} %get-tuple-element.67), channel_id=1, source_target_pairs={{0,16},{1,17},{2,18},{3,19},{4,20},{5,21},{6,22},{7,23},{8,24},{9,... | collective-permute-start | bytes 589832 | tf_op jit(solution)/shard_map/ppermute | solution.py:35
  5.7 18.5 %collective-permute-start.1 = (bf16[3,64,512]{2,1,0:T(8,128)(2,1)S(1)}, bf16[3,64,512]{2,1,0:T(8,128)(2,1)S(1)}, u32[]{:S(2)}, u32[]{:S(2)}) collective-permute-start(bf16[3,64,512]{2,1,0:T(8,128)(2,1)S(1)} %get-tuple-element.110), channel_id=1, source_target_pairs={{0,2},{1,3},{2,0},{3,1},{4,6},{5,7},{6,4},{7,5},{8,10},{9,11},{10,... | collective-permute-start | bytes 589832 | tf_op jit(solution)/shard_map/ppermute | solution.py:43
  13.6 9.8 %collective-permute-start = (s32[144]{0:T(256)S(1)}, s32[144]{0:T(256)S(1)}, u32[]{:S(2)}, u32[]{:S(2)}) collective-permute-start(s32[144]{0:T(256)S(1)} %slice_add_fusion), channel_id=1, source_target_pairs={{0,1},{1,2},{2,3},{3,4},{4,5},{5,6},{6,7},{7,8},{8,9},{9,10},{10,1... | collective-permute-start | bytes 1736 | tf_op jit(solution)/shard_map/ppermute | solution.py:365
  24.2 22.8 %collective-permute-start.10 = (bf16[3,64,512]{2,1,0:T(8,128)(2,1)S(1)}, bf16[3,64,512]{2,1,0:T(8,128)(2,1)}, u32[]{:S(2)}, u32[]{:S(2)}) collective-permute-start(bf16[3,64,512]{2,1,0:T(8,128)(2,1)S(1)} %collective-permute-done.1), channel_id=1, source_target_pairs={{0,12},{1,13},{2,14},{3,15},{4,0},{5,1},{6,2},{7,3},{8,4},{9,5},{1... | collective-permute-start | bytes 589832 | tf_op jit(solution)/shard_map/ppermute | solution.py:39
  24.3 23.0 %collective-permute-start.11 = (bf16[3,64,512]{2,1,0:T(8,128)(2,1)S(1)}, bf16[3,64,512]{2,1,0:T(8,128)(2,1)}, u32[]{:S(2)}, u32[]{:S(2)}) collective-permute-start(bf16[3,64,512]{2,1,0:T(8,128)(2,1)S(1)} %collective-permute-done.1), channel_id=1, source_target_pairs={{0,8},{1,9},{2,10},{3,11},{4,12},{5,13},{6,14},{7,15},{8,0},{9,1},... | collective-permute-start | bytes 589832 | tf_op jit(solution)/shard_map/ppermute | solution.py:39
  27.3 21.8 %collective-permute-start.12 = (bf16[3,64,512]{2,1,0:T(8,128)(2,1)S(1)}, bf16[3,64,512]{2,1,0:T(8,128)(2,1)}, u32[]{:S(2)}, u32[]{:S(2)}) collective-permute-start(bf16[3,64,512]{2,1,0:T(8,128)(2,1)S(1)} %collective-permute-done.1), channel_id=1, source_target_pairs={{0,4},{1,5},{2,6},{3,7},{4,8},{5,9},{6,10},{7,11},{8,12},{9,13},{1... | collective-permute-start | bytes 589832 | tf_op jit(solution)/shard_map/ppermute | solution.py:39
  42.7 15.7 %collective-permute-start.6 = (bf16[512,512]{1,0:T(8,128)(2,1)S(1)}, bf16[512,512]{1,0:T(8,128)(2,1)}, u32[]{:S(2)}, u32[]{:S(2)}) collective-permute-start(bf16[512,512]{1,0:T(8,128)(2,1)S(1)} %constant_dynamic-update-slice_fusion.refs_0_), channel_id=1, source_target_pairs={{0,64},{1,65},{4,68},{5,69},{8,72},{9,73},{12,76},{13,77},{16,80},... | collective-permute-start | bytes 1572872 | tf_op jit(solution)/shard_map/ppermute | solution.py:71
  43.7 14.7 %collective-permute-start.7 = (bf16[512,512]{1,0:T(8,128)(2,1)S(1)}, bf16[512,512]{1,0:T(8,128)(2,1)}, u32[]{:S(2)}, u32[]{:S(2)}) collective-permute-start(bf16[512,512]{1,0:T(8,128)(2,1)S(1)} %constant_dynamic-update-slice_fusion.refs_0_), channel_id=1, source_target_pairs={{0,194},{1,195},{4,198},{5,199},{8,202},{9,203},{12,206},{13,207},... | collective-permute-start | bytes 1572872 | tf_op jit(solution)/shard_map/ppermute | solution.py:71
  47.0 19.5 %collective-permute-start.14 = (bf16[4,3,64,512]{3,2,1,0:T(8,128)(2,1)S(1)}, bf16[4,3,64,512]{3,2,1,0:T(8,128)(2,1)}, u32[]{:S(2)}, u32[]{:S(2)}) collective-permute-start(bf16[4,3,64,512]{3,2,1,0:T(8,128)(2,1)S(1)} %pad_maximum_fusion.1.refs_1_), channel_id=1, source_target_pairs={{0,12},{1,13},{2,14},{3,15},{4,0},{5,1},{6,2},{7,3},{8,4},{9,5},{1... | collective-permute-start | bytes 2359304 | tf_op jit(solution)/shard_map/ppermute | solution.py:39
  47.3 19.7 %collective-permute-start.15 = (bf16[4,3,64,512]{3,2,1,0:T(8,128)(2,1)S(1)}, bf16[4,3,64,512]{3,2,1,0:T(8,128)(2,1)}, u32[]{:S(2)}, u32[]{:S(2)}) collective-permute-start(bf16[4,3,64,512]{3,2,1,0:T(8,128)(2,1)S(1)} %pad_maximum_fusion.1.refs_1_), channel_id=1, source_target_pairs={{0,4},{1,5},{2,6},{3,7},{4,8},{5,9},{6,10},{7,11},{8,12},{9,13},{1... | collective-permute-start | bytes 2359304 | tf_op jit(solution)/shard_map/ppermute | solution.py:39
  50.4 20.7 %collective-permute-start.13 = (bf16[4,3,64,512]{3,2,1,0:T(8,128)(2,1)S(1)}, bf16[4,3,64,512]{3,2,1,0:T(8,128)(2,1)}, u32[]{:S(2)}, u32[]{:S(2)}) collective-permute-start(bf16[4,3,64,512]{3,2,1,0:T(8,128)(2,1)S(1)} %pad_maximum_fusion.refs_2_), channel_id=1, source_target_pairs={{0,32},{1,33},{2,34},{3,35},{4,36},{5,37},{6,38},{7,39},{8,40},{9,... | collective-permute-start | bytes 2359304 | tf_op jit(solution)/shard_map/ppermute | solution.py:35
  58.4 15.2 %collective-permute-start.8 = (bf16[512,512]{1,0:T(8,128)(2,1)}, bf16[512,512]{1,0:T(8,128)(2,1)S(1)}, u32[]{:S(2)}, u32[]{:S(2)}) collective-permute-start(bf16[512,512]{1,0:T(8,128)(2,1)} %collective-permute-done.6.refs_0_), channel_id=1, source_target_pairs={{0,64},{1,65},{4,68},{5,69},{8,72},{9,73},{12,76},{13,77},{16,80},... | collective-permute-start | bytes 1572872 | tf_op jit(solution)/shard_map/ppermute | solution.py:71
  58.8 14.8 %collective-permute-start.9 = (bf16[512,512]{1,0:T(8,128)(2,1)}, bf16[512,512]{1,0:T(8,128)(2,1)S(1)}, u32[]{:S(2)}, u32[]{:S(2)}) collective-permute-start(bf16[512,512]{1,0:T(8,128)(2,1)} %collective-permute-done.7.refs_1_), channel_id=1, source_target_pairs={{0,194},{1,195},{4,198},{5,199},{8,202},{9,203},{12,206},{13,207},... | collective-permute-start | bytes 1572872 | tf_op jit(solution)/shard_map/ppermute | solution.py:71
  71.0 20.2 %collective-permute-start.20 = (bf16[4,3,64,512]{3,2,1,0:T(8,128)(2,1)S(1)}, bf16[4,3,64,512]{3,2,1,0:T(8,128)(2,1)S(1)}, u32[]{:S(2)}, u32[]{:S(2)}) collective-permute-start(bf16[4,3,64,512]{3,2,1,0:T(8,128)(2,1)S(1)} %pad_maximum_fusion.refs_2_), channel_id=1, source_target_pairs={{0,48},{1,49},{2,50},{3,51},{4,52},{5,53},{6,54},{7,55},{8,56},{9,... | collective-permute-start | bytes 2359304 | tf_op jit(solution)/shard_map/ppermute | solution.py:35
  73.6 19.0 %collective-permute-start.21 = (bf16[4,3,64,512]{3,2,1,0:T(8,128)(2,1)S(1)}, bf16[4,3,64,512]{3,2,1,0:T(8,128)(2,1)S(1)}, u32[]{:S(2)}, u32[]{:S(2)}) collective-permute-start(bf16[4,3,64,512]{3,2,1,0:T(8,128)(2,1)S(1)} %pad_maximum_fusion.refs_2_), channel_id=1, source_target_pairs={{0,16},{1,17},{2,18},{3,19},{4,20},{5,21},{6,22},{7,23},{8,24},{9,... | collective-permute-start | bytes 2359304 | tf_op jit(solution)/shard_map/ppermute | solution.py:35
  73.6 13.6 %collective-permute-start.16 = (bf16[512,512]{1,0:T(8,128)(2,1)S(1)}, bf16[512,512]{1,0:T(8,128)(2,1)S(1)}, u32[]{:S(2)}, u32[]{:S(2)}) collective-permute-start(bf16[512,512]{1,0:T(8,128)(2,1)S(1)} %collective-permute-done.8.refs_0_), channel_id=1, source_target_pairs={{0,64},{1,65},{4,68},{5,69},{8,72},{9,73},{12,76},{13,77},{16,80},... | collective-permute-start | bytes 1572872 | tf_op jit(solution)/shard_map/ppermute | solution.py:71
  73.7 13.5 %collective-permute-start.17 = (bf16[512,512]{1,0:T(8,128)(2,1)S(1)}, bf16[512,512]{1,0:T(8,128)(2,1)S(1)}, u32[]{:S(2)}, u32[]{:S(2)}) collective-permute-start(bf16[512,512]{1,0:T(8,128)(2,1)S(1)} %collective-permute-done.9.refs_1_), channel_id=1, source_target_pairs={{0,194},{1,195},{4,198},{5,199},{8,202},{9,203},{12,206},{13,207},... | collective-permute-start | bytes 1572872 | tf_op jit(solution)/shard_map/ppermute | solution.py:71
  76.9 18.8 %collective-permute-start.22 = (bf16[4,3,64,512]{3,2,1,0:T(8,128)(2,1)S(1)}, bf16[4,3,64,512]{3,2,1,0:T(8,128)(2,1)S(1)}, u32[]{:S(2)}, u32[]{:S(2)}) collective-permute-start(bf16[4,3,64,512]{3,2,1,0:T(8,128)(2,1)S(1)} %pad_maximum_fusion.1.refs_1_), channel_id=1, source_target_pairs={{0,8},{1,9},{2,10},{3,11},{4,12},{5,13},{6,14},{7,15},{8,0},{9,1},... | collective-permute-start | bytes 2359304 | tf_op jit(solution)/shard_map/ppermute | solution.py:39
  87.9 9.6 %collective-permute-start.18 = (bf16[256,512]{1,0:T(8,128)(2,1)S(1)}, bf16[256,512]{1,0:T(8,128)(2,1)S(1)}, u32[]{:S(2)}, u32[]{:S(2)}) collective-permute-start(bf16[256,512]{1,0:T(8,128)(2,1)S(1)} %get-tuple-element.82), channel_id=1, source_target_pairs={{0,64},{1,65},{4,68},{5,69},{8,72},{9,73},{12,76},{13,77},{16,80},... | collective-permute-start | bytes 786440 | tf_op jit(solution)/shard_map/ppermute | solution.py:71
  88.0 9.5 %collective-permute-start.19 = (bf16[256,512]{1,0:T(8,128)(2,1)S(1)}, bf16[256,512]{1,0:T(8,128)(2,1)S(1)}, u32[]{:S(2)}, u32[]{:S(2)}) collective-permute-start(bf16[256,512]{1,0:T(8,128)(2,1)S(1)} %get-tuple-element.83), channel_id=1, source_target_pairs={{0,194},{1,195},{4,198},{5,199},{8,202},{9,203},{12,206},{13,207},... | collective-permute-start | bytes 786440 | tf_op jit(solution)/shard_map/ppermute | solution.py:71
  113.1 5.5 %collective-permute-start.26 = (f32[16,512]{1,0:T(8,128)S(1)}, f32[16,512]{1,0:T(8,128)S(1)}, u32[]{:S(2)}, u32[]{:S(2)}) collective-permute-start(f32[16,512]{1,0:T(8,128)S(1)} %add_select_fusion.2), channel_id=1, source_target_pairs={{0,8},{1,9},{2,10},{3,11},{4,12},{5,13},{6,14},{7,15},{8,0},{9,1},... | collective-permute-start | bytes 98312 | tf_op jit(solution)/shard_map/ppermute | solution.py:446
  122.7 5.5 %collective-permute-start.28 = (f32[16,512]{1,0:T(8,128)S(1)}, f32[16,512]{1,0:T(8,128)S(1)}, u32[]{:S(2)}, u32[]{:S(2)}) collective-permute-start(f32[16,512]{1,0:T(8,128)S(1)} %add_select_fusion), channel_id=1, source_target_pairs={{0,32},{1,33},{2,34},{3,35},{4,36},{5,37},{6,38},{7,39},{8,40},{9,... | collective-permute-start | bytes 98312 | tf_op jit(solution)/shard_map/ppermute | solution.py:446
  (17 other events, 138.0 us)

commit v2 on v1

--- a/solution.py
+++ b/solution.py
@@ -221,15 +221,9 @@
 
 def li_kernel(which, a_ref, w_ref, out_ref):
     for t in range(3):
-
-        def step(m, _, t=t):
-            rows = pl.ds(pl.multiple_of(m * 256, 256), 256)
-            out_ref[t, rows, :] = jnp.dot(
-                a_ref[which, rows, :], w_ref[t], preferred_element_type=F32
-            ).astype(out_ref.dtype)
-            return 0
-
-        lax.fori_loop(0, 2, step, 0)
+        out_ref[t] = jnp.dot(
+            a_ref[which], w_ref[t], preferred_element_type=F32
+        ).astype(out_ref.dtype)
 
 
 def li_terms(which, a_full, w_full):
@@ -239,7 +233,7 @@
         out_shape=jax.ShapeDtypeStruct((3, 512, 512), BF16 if which else F32),
         in_specs=[vmem] * 2,
         out_specs=vmem,
-        compiler_params=pltpu.CompilerParams(vmem_limit_bytes=8 * 2**20),
+        compiler_params=pltpu.CompilerParams(vmem_limit_bytes=12 * 2**20),
         cost_estimate=pl.CostEstimate(
             flops=33 * 10**8, bytes_accessed=10 * 10**6, transcendentals=0
         ),
@@ -362,12 +356,12 @@
     total_len = ids.shape[0] * lax.axis_size(SEQ)
     tie = lax.optimization_barrier
 
-    halo = lax.ppermute(
-        ids[ids.shape[0] - HALO :] + 1, SEQ, [(i, i + 1) for i in range(len(COORDS) - 1)]
-    )
+    marks = ids[ids.shape[0] - HALO :] + 1
     weights = jnp.transpose(li_proj, (1, 0, 2))
     mine = lax.dynamic_slice_in_dim(weights, h * 512, 512, 2)
     theirs = lax.dynamic_slice_in_dim(weights, (1 - h) * 512, 512, 2)
+    mine, marks = tie((mine, marks))
+    halo = lax.ppermute(marks, SEQ, [(i, i + 1) for i in range(len(COORDS) - 1)])
     rows_b = from_run(theirs)
     ext_ids = jnp.concatenate([halo - 1, ids])[:, None]
     emb = jnp.transpose(embed_proj, (1, 0, 2))

time: 148 us -> 147 us (level)
  Pallas kernels: 30.4 us -> 28.9 us
    pallas_call x2, Pallas kernels: 8.46 us -> 6.88 us  [li_terms(): pl.pallas_call(functools.partial(li_kernel, which), out_shape=jax.ShapeDt...]
  transfers between devices with their start and end apart: 29 -> 29, of which waited for: 13 -> 13; matrix products, arithmetic and copies ran while one was open for 5% -> 5% of each run, Pallas kernels for 16% -> 15%
where the time goes in v2:
time: 147 us; the launch traced here: 146 us
  starting transfers between devices  48.7 us (33%)
  waiting for transfers between devices  38.4 us (26%)
  Pallas kernels  28.9 us (20%)
  blocking collectives  17 us (12%)
  other arithmetic  6.71 us (5%)
  local copies, waits for them, and re-layouts  5.76 us (4%)
    all_to_all x1, blocking collectives, shards(): terms = lax.all_to_all(terms, ('run', 'chan'), 0, 0, tiled=True)  17 us
    ppermute x8, starting transfers between devices, to_z(): return lax.ppermute(v, ('chan',) + SEQ, pairs)  13.2 us
    ppermute x4, waiting for transfers between devices, shards(): there = lax.ppermute(total, SEQ, swap)  9.85 us
    ppermute x6, starting transfers between devices, from_y(): lax.ppermute(v, SEQ, seq_pairs(lambda x, y, h, c: (x, (y - j) % NY, h, c)))  9.4 us
    ppermute x6, starting transfers between devices, from_x(): lax.ppermute(v, SEQ, seq_pairs(lambda x, y, h, c: ((x - j) % NX, y, h, c)))  9.16 us
    pallas_call x1, Pallas kernels, activations(): pl.pallas_call(act_kernel, grid=(4,), out_shape=(jax.ShapeDtypeStruct((25...  8.74 us
    pallas_call x6, Pallas kernels, gather(): pl.pallas_call(functools.partial(gather_kernel, steps, plan, halves), out...  8.73 us
    ppermute x6, waiting for transfers between devices, from_y(): lax.ppermute(v, SEQ, seq_pairs(lambda x, y, h, c: (x, (y - j) % NY, h, c)))  8.53 us
  transfers between devices with their start and end apart: 29, of which 13 were waited for; matrix products, arithmetic and copies ran while one was open for 5% of the time, Pallas kernels for 15%

profile of v2, /device:TPU:8, one launch (start us, length us, event | category | flops | bytes accessed | tf_op | source)
XLA Modules:
  0.0 146.0 jit_solution(6135457998171418781)
XLA Ops:
  1.9 2.8 %collective-permute-start.2 = (bf16[3,64,512]{2,1,0:T(8,128)(2,1)S(1)}, bf16[3,64,512]{2,1,0:T(8,128)(2,1)S(1)}, u32[]{:S(2)}, u32[]{:S(2)}) collective-permute-start(bf16[3,64,512]{2,1,0:T(8,128)(2,1)S(1)} %get-tuple-element.71), channel_id=1, source_target_pairs={{0,48},{1,49},{2,50},{3,51},{4,52},{5,53},{6,54},{7,55},{8,56},{9,... | collective-permute-start | bytes 589832 | tf_op jit(solution)/shard_map/ppermute | solution.py:35
  6.4 7.2 %collective-permute-start.1 = (bf16[3,64,512]{2,1,0:T(8,128)(2,1)S(1)}, bf16[3,64,512]{2,1,0:T(8,128)(2,1)S(1)}, u32[]{:S(2)}, u32[]{:S(2)}) collective-permute-start(bf16[3,64,512]{2,1,0:T(8,128)(2,1)S(1)} %get-tuple-element.113), channel_id=1, source_target_pairs={{0,2},{1,3},{2,0},{3,1},{4,6},{5,7},{6,4},{7,5},{8,10},{9,11},{10,... | collective-permute-start | bytes 589832 | tf_op jit(solution)/shard_map/ppermute | solution.py:43
  16.7 6.7 %collective-permute-done = s32[144]{0:T(256)S(1)} collective-permute-done((s32[144]{0:T(256)S(1)}, s32[144]{0:T(256)S(1)}, u32[]{:S(2)}, u32[]{:S(2)}) %collective-permute-start) | collective-permute-done | bytes 608 | tf_op jit(solution)/shard_map/ppermute | solution.py:364
  24.3 3.1 %collective-permute-start.11 = (bf16[3,64,512]{2,1,0:T(8,128)(2,1)S(1)}, bf16[3,64,512]{2,1,0:T(8,128)(2,1)}, u32[]{:S(2)}, u32[]{:S(2)}) collective-permute-start(bf16[3,64,512]{2,1,0:T(8,128)(2,1)S(1)} %collective-permute-done.1), channel_id=1, source_target_pairs={{0,8},{1,9},{2,10},{3,11},{4,12},{5,13},{6,14},{7,15},{8,0},{9,1},... | collective-permute-start | bytes 589832 | tf_op jit(solution)/shard_map/ppermute | solution.py:39
  32.1 8.7 %shard_map.82 = (bf16[256,512]{1,0:T(8,128)(2,1)S(1)}, bf16[256,512]{1,0:T(8,128)(2,1)S(1)}) custom-call(s32[5]{0:T(128)S(1)} %stack.62.where, s32[400,1]{1,0:T(8,128)S(1)} %copy.29.ids_ref, bf16[3,512,1024]{2,1,0:T(8,128)(2,1)S(1)} %bitcast.51, f32[3,7,1024]{2,1,0:T(8,128)S(1)} %bitcast.52, f32[64,256]{1,0:T(8,128)S(1)} %pad.4.mr_ref), custom_call_target="tpu_custom_call" | custom-call | flops 4000000000 | bytes 8000000 | tf_op jit(solution)/shard_map/pallas_call | solution.py:136
  43.7 2.3 %collective-permute-start.7 = (bf16[512,512]{1,0:T(8,128)(2,1)S(1)}, bf16[512,512]{1,0:T(8,128)(2,1)}, u32[]{:S(2)}, u32[]{:S(2)}) collective-permute-start(bf16[512,512]{1,0:T(8,128)(2,1)S(1)} %constant_dynamic-update-slice_fusion.refs_0_), channel_id=1, source_target_pairs={{0,194},{1,195},{4,198},{5,199},{8,202},{9,203},{12,206},{13,207},... | collective-permute-start | bytes 1572872 | tf_op jit(solution)/shard_map/ppermute | solution.py:71
  53.7 4.7 %collective-permute-done.6.refs_0_ = bf16[512,512]{1,0:T(8,128)(2,1)} collective-permute-done((bf16[512,512]{1,0:T(8,128)(2,1)S(1)}, bf16[512,512]{1,0:T(8,128)(2,1)}, u32[]{:S(2)}, u32[]{:S(2)}) %collective-permute-start.6) | collective-permute-done | bytes 524320 | tf_op jit(solution)/shard_map/ppermute | solution.py:71
  58.8 2.8 %collective-permute-start.9 = (bf16[512,512]{1,0:T(8,128)(2,1)}, bf16[512,512]{1,0:T(8,128)(2,1)S(1)}, u32[]{:S(2)}, u32[]{:S(2)}) collective-permute-start(bf16[512,512]{1,0:T(8,128)(2,1)} %collective-permute-done.7.refs_1_), channel_id=1, source_target_pairs={{0,194},{1,195},{4,198},{5,199},{8,202},{9,203},{12,206},{13,207},... | collective-permute-start | bytes 1572872 | tf_op jit(solution)/shard_map/ppermute | solution.py:71
  61.6 5.0 %collective-permute-done.14.refs_3_ = bf16[4,3,64,512]{3,2,1,0:T(8,128)(2,1)} collective-permute-done((bf16[4,3,64,512]{3,2,1,0:T(8,128)(2,1)S(1)}, bf16[4,3,64,512]{3,2,1,0:T(8,128)(2,1)}, u32[]{:S(2)}, u32[]{:S(2)}) %collective-permute-start.14) | collective-permute-done | bytes 786464 | tf_op jit(solution)/shard_map/ppermute | solution.py:39
  67.0 4.1 %collective-permute-done.13.refs_2_ = bf16[4,3,64,512]{3,2,1,0:T(8,128)(2,1)} collective-permute-done((bf16[4,3,64,512]{3,2,1,0:T(8,128)(2,1)S(1)}, bf16[4,3,64,512]{3,2,1,0:T(8,128)(2,1)}, u32[]{:S(2)}, u32[]{:S(2)}) %collective-permute-start.13) | collective-permute-done | bytes 786464 | tf_op jit(solution)/shard_map/ppermute | solution.py:35
  71.0 2.5 %collective-permute-start.20 = (bf16[4,3,64,512]{3,2,1,0:T(8,128)(2,1)S(1)}, bf16[4,3,64,512]{3,2,1,0:T(8,128)(2,1)S(1)}, u32[]{:S(2)}, u32[]{:S(2)}) collective-permute-start(bf16[4,3,64,512]{3,2,1,0:T(8,128)(2,1)S(1)} %pad_maximum_fusion.refs_2_), channel_id=1, source_target_pairs={{0,48},{1,49},{2,50},{3,51},{4,52},{5,53},{6,54},{7,55},{8,56},{9,... | collective-permute-start | bytes 2359304 | tf_op jit(solution)/shard_map/ppermute | solution.py:35
  73.8 3.1 %collective-permute-start.17 = (bf16[512,512]{1,0:T(8,128)(2,1)S(1)}, bf16[512,512]{1,0:T(8,128)(2,1)S(1)}, u32[]{:S(2)}, u32[]{:S(2)}) collective-permute-start(bf16[512,512]{1,0:T(8,128)(2,1)S(1)} %collective-permute-done.9.refs_1_), channel_id=1, source_target_pairs={{0,194},{1,195},{4,198},{5,199},{8,202},{9,203},{12,206},{13,207},... | collective-permute-start | bytes 1572872 | tf_op jit(solution)/shard_map/ppermute | solution.py:71
  76.9 2.3 %collective-permute-start.22 = (bf16[4,3,64,512]{3,2,1,0:T(8,128)(2,1)S(1)}, bf16[4,3,64,512]{3,2,1,0:T(8,128)(2,1)S(1)}, u32[]{:S(2)}, u32[]{:S(2)}) collective-permute-start(bf16[4,3,64,512]{3,2,1,0:T(8,128)(2,1)S(1)} %pad_maximum_fusion.1.refs_1_), channel_id=1, source_target_pairs={{0,8},{1,9},{2,10},{3,11},{4,12},{5,13},{6,14},{7,15},{8,0},{9,1},... | collective-permute-start | bytes 2359304 | tf_op jit(solution)/shard_map/ppermute | solution.py:39
  82.0 2.9 %shard_map.85 = (bf16[2,512,2048]{2,1,0:T(8,128)(2,1)S(1)}, bf16[3,2048,512]{2,1,0:T(8,128)(2,1)S(1)}) custom-call(s32[5]{0:T(128)S(1)} %stack.62.where, bf16[512,512]{1,0:T(8,128)(2,1)S(1)} %collective-permute-done.8.refs_0_, bf16[512,512]{1,0:T(8,128)(2,1)S(1)} %collective-permute-done.9.refs_1_, ...), custom_call_target="tpu_custom_call", output_to_operand_aliasing={{0}: (6, {}), {1}: (7, {})} | custom-call | flops 1000000 | bytes 6000000 | tf_op jit(solution)/shard_map/pallas_call | solution.py:210
  84.9 2.3 %collective-permute-done.16.refs_0_ = bf16[512,512]{1,0:T(8,128)(2,1)S(1)} collective-permute-done((bf16[512,512]{1,0:T(8,128)(2,1)S(1)}, bf16[512,512]{1,0:T(8,128)(2,1)S(1)}, u32[]{:S(2)}, u32[]{:S(2)}) %collective-permute-start.16) | collective-permute-done | bytes 524320 | tf_op jit(solution)/shard_map/ppermute | solution.py:71
  88.2 3.0 %collective-permute-start.19 = (bf16[256,512]{1,0:T(8,128)(2,1)S(1)}, bf16[256,512]{1,0:T(8,128)(2,1)S(1)}, u32[]{:S(2)}, u32[]{:S(2)}) collective-permute-start(bf16[256,512]{1,0:T(8,128)(2,1)S(1)} %get-tuple-element.87), channel_id=1, source_target_pairs={{0,194},{1,195},{4,198},{5,199},{8,202},{9,203},{12,206},{13,207},... | collective-permute-start | bytes 786440 | tf_op jit(solution)/shard_map/ppermute | solution.py:71
  92.6 3.2 %collective-permute-done.22.refs_2_ = bf16[4,3,64,512]{3,2,1,0:T(8,128)(2,1)S(1)} collective-permute-done((bf16[4,3,64,512]{3,2,1,0:T(8,128)(2,1)S(1)}, bf16[4,3,64,512]{3,2,1,0:T(8,128)(2,1)S(1)}, u32[]{:S(2)}, u32[]{:S(2)}) %collective-permute-start.22) | collective-permute-done | bytes 786464 | tf_op jit(solution)/shard_map/ppermute | solution.py:39
  98.1 3.4 %shard_map.90 = bf16[3,512,512]{2,1,0:T(8,128)(2,1)S(1)} custom-call(bf16[2,512,2048]{2,1,0:T(8,128)(2,1)S(1)} %get-tuple-element.94.a_ref, bf16[3,2048,512]{2,1,0:T(8,128)(2,1)S(1)} %get-tuple-element.95.w_ref), custom_call_target="tpu_custom_call" | custom-call | flops 3300000000 | bytes 10000000 | tf_op jit(solution)/shard_map/pallas_call | solution.py:231
  101.9 3.4 %shard_map.89.own_ref = f32[3,512,512]{2,1,0:T(8,128)S(1)} custom-call(bf16[2,512,2048]{2,1,0:T(8,128)(2,1)S(1)} %get-tuple-element.94.a_ref, bf16[3,2048,512]{2,1,0:T(8,128)(2,1)S(1)} %get-tuple-element.95.w_ref), custom_call_target="tpu_custom_call" | custom-call | flops 3300000000 | bytes 10000000 | tf_op jit(solution)/shard_map/pallas_call | solution.py:231
  108.2 3.4 %collective-permute-done.25 = f32[16,512]{1,0:T(8,128)S(1)} collective-permute-done((f32[16,512]{1,0:T(8,128)S(1)}, f32[16,512]{1,0:T(8,128)S(1)}, u32[]{:S(2)}, u32[]{:S(2)}) %collective-permute-start.25) | collective-permute-done | bytes 32800 | tf_op jit(solution)/shard_map/ppermute | solution.py:440
  113.7 3.4 %collective-permute-done.26 = f32[16,512]{1,0:T(8,128)S(1)} collective-permute-done((f32[16,512]{1,0:T(8,128)S(1)}, f32[16,512]{1,0:T(8,128)S(1)}, u32[]{:S(2)}, u32[]{:S(2)}) %collective-permute-start.26) | collective-permute-done | bytes 32800 | tf_op jit(solution)/shard_map/ppermute | solution.py:440
  121.2 2.3 %collective-permute-start.28 = (f32[16,512]{1,0:T(8,128)S(1)}, f32[16,512]{1,0:T(8,128)S(1)}, u32[]{:S(2)}, u32[]{:S(2)}) collective-permute-start(f32[16,512]{1,0:T(8,128)S(1)} %add_select_fusion), channel_id=1, source_target_pairs={{0,32},{1,33},{2,34},{3,35},{4,36},{5,37},{6,38},{7,39},{8,40},{9,... | collective-permute-start | bytes 98312 | tf_op jit(solution)/shard_map/ppermute | solution.py:440
  123.5 2.3 %shard_map.92.inner_ref = f32[512,512]{1,0:T(8,128)S(1)} custom-call(bf16[512,512]{1,0:T(8,128)(2,1)S(1)} %get-tuple-element.105.x_ref, f32[32,512]{1,0:T(8,128)S(1)} %broadcast_select_fusion.h_ref), custom_call_target="tpu_custom_call" | custom-call | flops 4300000256 | bytes 2000000 | tf_op jit(solution)/shard_map/pallas_call | solution.py:296
  128.3 17.0 %all_to_all.5 = bf16[8,256,128]{2,1,0:T(8,128)(2,1)S(1)} all-to-all(bf16[8,256,128]{2,1,0:T(8,128)(2,1)S(1)} %shard_map.93), channel_id=1, replica_groups=mesh['chan'=4,'x'=4,'y'=4,'run'=2,'core'=2] {'run','chan'}, dimensions={0} | all-to-all | bytes 1048576 | tf_op jit(solution)/shard_map/all_to_all | solution.py:451
  (109 shorter events, 43.3 us)
Async XLA Ops:
  1.9 22.3 %collective-permute-start.2 = (bf16[3,64,512]{2,1,0:T(8,128)(2,1)S(1)}, bf16[3,64,512]{2,1,0:T(8,128)(2,1)S(1)}, u32[]{:S(2)}, u32[]{:S(2)}) collective-permute-start(bf16[3,64,512]{2,1,0:T(8,128)(2,1)S(1)} %get-tuple-element.71), channel_id=1, source_target_pairs={{0,48},{1,49},{2,50},{3,51},{4,52},{5,53},{6,54},{7,55},{8,56},{9,... | collective-permute-start | bytes 589832 | tf_op jit(solution)/shard_map/ppermute | solution.py:35
  4.7 19.4 %collective-permute-start.3 = (bf16[3,64,512]{2,1,0:T(8,128)(2,1)S(1)}, bf16[3,64,512]{2,1,0:T(8,128)(2,1)S(1)}, u32[]{:S(2)}, u32[]{:S(2)}) collective-permute-start(bf16[3,64,512]{2,1,0:T(8,128)(2,1)S(1)} %get-tuple-element.71), channel_id=1, source_target_pairs={{0,32},{1,33},{2,34},{3,35},{4,36},{5,37},{6,38},{7,39},{8,40},{9,... | collective-permute-start | bytes 589832 | tf_op jit(solution)/shard_map/ppermute | solution.py:35
  5.5 18.6 %collective-permute-start.4 = (bf16[3,64,512]{2,1,0:T(8,128)(2,1)S(1)}, bf16[3,64,512]{2,1,0:T(8,128)(2,1)S(1)}, u32[]{:S(2)}, u32[]{:S(2)}) collective-permute-start(bf16[3,64,512]{2,1,0:T(8,128)(2,1)S(1)} %get-tuple-element.71), channel_id=1, source_target_pairs={{0,16},{1,17},{2,18},{3,19},{4,20},{5,21},{6,22},{7,23},{8,24},{9,... | collective-permute-start | bytes 589832 | tf_op jit(solution)/shard_map/ppermute | solution.py:35
  6.4 17.8 %collective-permute-start.1 = (bf16[3,64,512]{2,1,0:T(8,128)(2,1)S(1)}, bf16[3,64,512]{2,1,0:T(8,128)(2,1)S(1)}, u32[]{:S(2)}, u32[]{:S(2)}) collective-permute-start(bf16[3,64,512]{2,1,0:T(8,128)(2,1)S(1)} %get-tuple-element.113), channel_id=1, source_target_pairs={{0,2},{1,3},{2,0},{3,1},{4,6},{5,7},{6,4},{7,5},{8,10},{9,11},{10,... | collective-permute-start | bytes 589832 | tf_op jit(solution)/shard_map/ppermute | solution.py:43
  13.6 9.8 %collective-permute-start = (s32[144]{0:T(256)S(1)}, s32[144]{0:T(256)S(1)}, u32[]{:S(2)}, u32[]{:S(2)}) collective-permute-start(s32[144]{0:T(256)S(1)} %slice_add_fusion), channel_id=1, source_target_pairs={{0,1},{1,2},{2,3},{3,4},{4,5},{5,6},{6,7},{7,8},{8,9},{9,10},{10,1... | collective-permute-start | bytes 1736 | tf_op jit(solution)/shard_map/ppermute | solution.py:364
  24.2 22.8 %collective-permute-start.10 = (bf16[3,64,512]{2,1,0:T(8,128)(2,1)S(1)}, bf16[3,64,512]{2,1,0:T(8,128)(2,1)}, u32[]{:S(2)}, u32[]{:S(2)}) collective-permute-start(bf16[3,64,512]{2,1,0:T(8,128)(2,1)S(1)} %collective-permute-done.1), channel_id=1, source_target_pairs={{0,12},{1,13},{2,14},{3,15},{4,0},{5,1},{6,2},{7,3},{8,4},{9,5},{1... | collective-permute-start | bytes 589832 | tf_op jit(solution)/shard_map/ppermute | solution.py:39
  24.3 23.0 %collective-permute-start.11 = (bf16[3,64,512]{2,1,0:T(8,128)(2,1)S(1)}, bf16[3,64,512]{2,1,0:T(8,128)(2,1)}, u32[]{:S(2)}, u32[]{:S(2)}) collective-permute-start(bf16[3,64,512]{2,1,0:T(8,128)(2,1)S(1)} %collective-permute-done.1), channel_id=1, source_target_pairs={{0,8},{1,9},{2,10},{3,11},{4,12},{5,13},{6,14},{7,15},{8,0},{9,1},... | collective-permute-start | bytes 589832 | tf_op jit(solution)/shard_map/ppermute | solution.py:39
  27.3 21.8 %collective-permute-start.12 = (bf16[3,64,512]{2,1,0:T(8,128)(2,1)S(1)}, bf16[3,64,512]{2,1,0:T(8,128)(2,1)}, u32[]{:S(2)}, u32[]{:S(2)}) collective-permute-start(bf16[3,64,512]{2,1,0:T(8,128)(2,1)S(1)} %collective-permute-done.1), channel_id=1, source_target_pairs={{0,4},{1,5},{2,6},{3,7},{4,8},{5,9},{6,10},{7,11},{8,12},{9,13},{1... | collective-permute-start | bytes 589832 | tf_op jit(solution)/shard_map/ppermute | solution.py:39
  42.7 15.7 %collective-permute-start.6 = (bf16[512,512]{1,0:T(8,128)(2,1)S(1)}, bf16[512,512]{1,0:T(8,128)(2,1)}, u32[]{:S(2)}, u32[]{:S(2)}) collective-permute-start(bf16[512,512]{1,0:T(8,128)(2,1)S(1)} %constant_dynamic-update-slice_fusion.refs_0_), channel_id=1, source_target_pairs={{0,64},{1,65},{4,68},{5,69},{8,72},{9,73},{12,76},{13,77},{16,80},... | collective-permute-start | bytes 1572872 | tf_op jit(solution)/shard_map/ppermute | solution.py:71
  43.7 14.7 %collective-permute-start.7 = (bf16[512,512]{1,0:T(8,128)(2,1)S(1)}, bf16[512,512]{1,0:T(8,128)(2,1)}, u32[]{:S(2)}, u32[]{:S(2)}) collective-permute-start(bf16[512,512]{1,0:T(8,128)(2,1)S(1)} %constant_dynamic-update-slice_fusion.refs_0_), channel_id=1, source_target_pairs={{0,194},{1,195},{4,198},{5,199},{8,202},{9,203},{12,206},{13,207},... | collective-permute-start | bytes 1572872 | tf_op jit(solution)/shard_map/ppermute | solution.py:71
  47.0 19.5 %collective-permute-start.14 = (bf16[4,3,64,512]{3,2,1,0:T(8,128)(2,1)S(1)}, bf16[4,3,64,512]{3,2,1,0:T(8,128)(2,1)}, u32[]{:S(2)}, u32[]{:S(2)}) collective-permute-start(bf16[4,3,64,512]{3,2,1,0:T(8,128)(2,1)S(1)} %pad_maximum_fusion.1.refs_1_), channel_id=1, source_target_pairs={{0,12},{1,13},{2,14},{3,15},{4,0},{5,1},{6,2},{7,3},{8,4},{9,5},{1... | collective-permute-start | bytes 2359304 | tf_op jit(solution)/shard_map/ppermute | solution.py:39
  47.3 19.7 %collective-permute-start.15 = (bf16[4,3,64,512]{3,2,1,0:T(8,128)(2,1)S(1)}, bf16[4,3,64,512]{3,2,1,0:T(8,128)(2,1)}, u32[]{:S(2)}, u32[]{:S(2)}) collective-permute-start(bf16[4,3,64,512]{3,2,1,0:T(8,128)(2,1)S(1)} %pad_maximum_fusion.1.refs_1_), channel_id=1, source_target_pairs={{0,4},{1,5},{2,6},{3,7},{4,8},{5,9},{6,10},{7,11},{8,12},{9,13},{1... | collective-permute-start | bytes 2359304 | tf_op jit(solution)/shard_map/ppermute | solution.py:39
  50.4 20.7 %collective-permute-start.13 = (bf16[4,3,64,512]{3,2,1,0:T(8,128)(2,1)S(1)}, bf16[4,3,64,512]{3,2,1,0:T(8,128)(2,1)}, u32[]{:S(2)}, u32[]{:S(2)}) collective-permute-start(bf16[4,3,64,512]{3,2,1,0:T(8,128)(2,1)S(1)} %pad_maximum_fusion.refs_2_), channel_id=1, source_target_pairs={{0,32},{1,33},{2,34},{3,35},{4,36},{5,37},{6,38},{7,39},{8,40},{9,... | collective-permute-start | bytes 2359304 | tf_op jit(solution)/shard_map/ppermute | solution.py:35
  58.4 15.2 %collective-permute-start.8 = (bf16[512,512]{1,0:T(8,128)(2,1)}, bf16[512,512]{1,0:T(8,128)(2,1)S(1)}, u32[]{:S(2)}, u32[]{:S(2)}) collective-permute-start(bf16[512,512]{1,0:T(8,128)(2,1)} %collective-permute-done.6.refs_0_), channel_id=1, source_target_pairs={{0,64},{1,65},{4,68},{5,69},{8,72},{9,73},{12,76},{13,77},{16,80},... | collective-permute-start | bytes 1572872 | tf_op jit(solution)/shard_map/ppermute | solution.py:71
  58.8 14.8 %collective-permute-start.9 = (bf16[512,512]{1,0:T(8,128)(2,1)}, bf16[512,512]{1,0:T(8,128)(2,1)S(1)}, u32[]{:S(2)}, u32[]{:S(2)}) collective-permute-start(bf16[512,512]{1,0:T(8,128)(2,1)} %collective-permute-done.7.refs_1_), channel_id=1, source_target_pairs={{0,194},{1,195},{4,198},{5,199},{8,202},{9,203},{12,206},{13,207},... | collective-permute-start | bytes 1572872 | tf_op jit(solution)/shard_map/ppermute | solution.py:71
  71.0 20.2 %collective-permute-start.20 = (bf16[4,3,64,512]{3,2,1,0:T(8,128)(2,1)S(1)}, bf16[4,3,64,512]{3,2,1,0:T(8,128)(2,1)S(1)}, u32[]{:S(2)}, u32[]{:S(2)}) collective-permute-start(bf16[4,3,64,512]{3,2,1,0:T(8,128)(2,1)S(1)} %pad_maximum_fusion.refs_2_), channel_id=1, source_target_pairs={{0,48},{1,49},{2,50},{3,51},{4,52},{5,53},{6,54},{7,55},{8,56},{9,... | collective-permute-start | bytes 2359304 | tf_op jit(solution)/shard_map/ppermute | solution.py:35
  73.6 19.0 %collective-permute-start.21 = (bf16[4,3,64,512]{3,2,1,0:T(8,128)(2,1)S(1)}, bf16[4,3,64,512]{3,2,1,0:T(8,128)(2,1)S(1)}, u32[]{:S(2)}, u32[]{:S(2)}) collective-permute-start(bf16[4,3,64,512]{3,2,1,0:T(8,128)(2,1)S(1)} %pad_maximum_fusion.refs_2_), channel_id=1, source_target_pairs={{0,16},{1,17},{2,18},{3,19},{4,20},{5,21},{6,22},{7,23},{8,24},{9,... | collective-permute-start | bytes 2359304 | tf_op jit(solution)/shard_map/ppermute | solution.py:35
  73.6 13.6 %collective-permute-start.16 = (bf16[512,512]{1,0:T(8,128)(2,1)S(1)}, bf16[512,512]{1,0:T(8,128)(2,1)S(1)}, u32[]{:S(2)}, u32[]{:S(2)}) collective-permute-start(bf16[512,512]{1,0:T(8,128)(2,1)S(1)} %collective-permute-done.8.refs_0_), channel_id=1, source_target_pairs={{0,64},{1,65},{4,68},{5,69},{8,72},{9,73},{12,76},{13,77},{16,80},... | collective-permute-start | bytes 1572872 | tf_op jit(solution)/shard_map/ppermute | solution.py:71
  73.8 13.4 %collective-permute-start.17 = (bf16[512,512]{1,0:T(8,128)(2,1)S(1)}, bf16[512,512]{1,0:T(8,128)(2,1)S(1)}, u32[]{:S(2)}, u32[]{:S(2)}) collective-permute-start(bf16[512,512]{1,0:T(8,128)(2,1)S(1)} %collective-permute-done.9.refs_1_), channel_id=1, source_target_pairs={{0,194},{1,195},{4,198},{5,199},{8,202},{9,203},{12,206},{13,207},... | collective-permute-start | bytes 1572872 | tf_op jit(solution)/shard_map/ppermute | solution.py:71
  76.9 18.8 %collective-permute-start.22 = (bf16[4,3,64,512]{3,2,1,0:T(8,128)(2,1)S(1)}, bf16[4,3,64,512]{3,2,1,0:T(8,128)(2,1)S(1)}, u32[]{:S(2)}, u32[]{:S(2)}) collective-permute-start(bf16[4,3,64,512]{3,2,1,0:T(8,128)(2,1)S(1)} %pad_maximum_fusion.1.refs_1_), channel_id=1, source_target_pairs={{0,8},{1,9},{2,10},{3,11},{4,12},{5,13},{6,14},{7,15},{8,0},{9,1},... | collective-permute-start | bytes 2359304 | tf_op jit(solution)/shard_map/ppermute | solution.py:39
  87.9 9.6 %collective-permute-start.18 = (bf16[256,512]{1,0:T(8,128)(2,1)S(1)}, bf16[256,512]{1,0:T(8,128)(2,1)S(1)}, u32[]{:S(2)}, u32[]{:S(2)}) collective-permute-start(bf16[256,512]{1,0:T(8,128)(2,1)S(1)} %get-tuple-element.86), channel_id=1, source_target_pairs={{0,64},{1,65},{4,68},{5,69},{8,72},{9,73},{12,76},{13,77},{16,80},... | collective-permute-start | bytes 786440 | tf_op jit(solution)/shard_map/ppermute | solution.py:71
  88.2 9.3 %collective-permute-start.19 = (bf16[256,512]{1,0:T(8,128)(2,1)S(1)}, bf16[256,512]{1,0:T(8,128)(2,1)S(1)}, u32[]{:S(2)}, u32[]{:S(2)}) collective-permute-start(bf16[256,512]{1,0:T(8,128)(2,1)S(1)} %get-tuple-element.87), channel_id=1, source_target_pairs={{0,194},{1,195},{4,198},{5,199},{8,202},{9,203},{12,206},{13,207},... | collective-permute-start | bytes 786440 | tf_op jit(solution)/shard_map/ppermute | solution.py:71
  111.6 5.5 %collective-permute-start.26 = (f32[16,512]{1,0:T(8,128)S(1)}, f32[16,512]{1,0:T(8,128)S(1)}, u32[]{:S(2)}, u32[]{:S(2)}) collective-permute-start(f32[16,512]{1,0:T(8,128)S(1)} %add_select_fusion.2), channel_id=1, source_target_pairs={{0,8},{1,9},{2,10},{3,11},{4,12},{5,13},{6,14},{7,15},{8,0},{9,1},... | collective-permute-start | bytes 98312 | tf_op jit(solution)/shard_map/ppermute | solution.py:440
  121.2 5.5 %collective-permute-start.28 = (f32[16,512]{1,0:T(8,128)S(1)}, f32[16,512]{1,0:T(8,128)S(1)}, u32[]{:S(2)}, u32[]{:S(2)}) collective-permute-start(f32[16,512]{1,0:T(8,128)S(1)} %add_select_fusion), channel_id=1, source_target_pairs={{0,32},{1,33},{2,34},{3,35},{4,36},{5,37},{6,38},{7,39},{8,40},{9,... | collective-permute-start | bytes 98312 | tf_op jit(solution)/shard_map/ppermute | solution.py:440
  (17 other events, 136.9 us)
